TPU v7x, 128 devices: a whole 4x4x4 slice. The times are simulated.
128 devices in a mesh: section: 2 (over core), dp: 16 (over z, y), tensor: 4 (over x).
Axes of the slice: x: 4, y: 4, z: 4, core: 2. Of those that a mesh axis runs over, the one named last changes fastest.
Arguments:
- inputs: bfloat16 [2, 4096, 1024], P(None, ('dp', 'tensor')), may hold values from -6 to 6
- cotangent: bfloat16 [2, 4096, 1024], P(None, ('dp', 'tensor')), may hold values from -6 to 6
- w_qkv: bfloat16 [2, 1024, 3, 1024], P('section', 'dp', None, 'tensor'), may hold values from -0.25 to 0.25
- b_qkv: float32 [2, 3, 1024], P('section', None, 'tensor'), may hold values from -2 to 2
- w_out: bfloat16 [2, 1024, 1024], P('section', 'tensor', 'dp'), may hold values from -0.5 to 0.5
- w_fc: bfloat16 [2, 1024, 4096], P('section', 'dp', 'tensor'), may hold values from -0.1875 to 0.1875
- b_fc: float32 [2, 4096], P('section', 'tensor'), may hold values from -3 to 3
- w_proj: bfloat16 [2, 4096, 1024], P('section', 'tensor', 'dp'), may hold values from -0.09375 to 0.09375
- norm_gains: float32 [2, 2, 1024], P('section'), may hold values from 0.1 to 1.9
- norm_shifts: float32 [2, 4, 1024], P('section'), may hold values from -2 to 2
- seq_lengths: int32 [64], replicated, may hold values from 1 to 256, as said below
- seq_ranks: int32 [64], replicated, may hold values from 0 to 15
- seq_micros: int32 [64], replicated, may hold values from 0 to 1
Outputs:
- activations: bfloat16 [2, 2, 4096, 1024], P('section', None, ('dp', 'tensor'))
- input_grads: bfloat16 [2, 2, 4096, 1024], P('section', None, ('dp', 'tensor'))
- grad_w_qkv: float32 [2, 1024, 3, 1024], P('section', 'dp', None, 'tensor')
- grad_b_qkv: float32 [2, 3, 1024], P('section', None, 'tensor')
- grad_w_out: float32 [2, 1024, 1024], P('section', 'tensor', 'dp')
- grad_w_fc: float32 [2, 1024, 4096], P('section', 'dp', 'tensor')
- grad_b_fc: float32 [2, 4096], P('section', 'tensor')
- grad_w_proj: float32 [2, 4096, 1024], P('section', 'tensor', 'dp')
- grad_norm_gains: float32 [2, 2, 1024], P('section')
- grad_norm_shifts: float32 [2, 4, 1024], P('section')
Inputs may be any that keep to these rules, and one draw needn't show every extreme that they name: `seq_lengths`: the sequences of one slot (data rank and micro-batch) hold at most 256 tokens together and fill its rows in order of their index; every slot holds one or more sequences; in every draw one sequence, alone in its slot, has exactly 256 tokens.
All inputs are finite; a program needn't handle non-finite values.
Results may differ from a plain program's by a relative error of at most 0.035.
Values may be sent and summed in bfloat16 or wider, within the bound.
A program may use at most 128 MiB of HBM per device.

v0:
```python
from functools import partial

import jax
import jax.numpy as jnp
from jax import lax
from jax.sharding import PartitionSpec as P

HD = 64


epsilon = 1e-05


def passed_along(block, axis, distance):
    devices = range(lax.axis_size(axis))
    route = [(i - distance, i) for i in devices if i - distance in devices]
    return lax.ppermute(block, axis, route)


def slot_labels(lengths, ranks, micros, rank_now, micro_now, row_count):
    mine = (ranks == rank_now) & (micros == micro_now)
    taken = jnp.where(mine, lengths, 0)
    ends = jnp.cumsum(taken, dtype=jnp.int32)
    starts = ends - taken
    places = jnp.arange(row_count, dtype=jnp.int32)[:, None]
    inside = mine[None, :] & (places >= starts[None, :]) & (places < ends[None, :])
    numbers = jnp.arange(lengths.shape[0], dtype=jnp.int32)[None, :] + 1
    return jnp.sum(jnp.where(inside, numbers, 0), axis=1, dtype=jnp.int32) - 1


def allowed(label_rows, label_cols, place_rows, place_cols):
    same = (label_rows[:, None] == label_cols[None, :]) & (label_rows[:, None] >= 0)
    causal = place_cols[None, :] <= place_rows[:, None]
    return same & causal | (place_rows[:, None] == place_cols[None, :])


def norm_forward(values, gain_row, shift_row):
    average = jnp.mean(values, axis=-1, keepdims=True)
    centered = values - average
    inv_std = lax.rsqrt(jnp.mean(centered * centered, axis=-1, keepdims=True) + epsilon)
    normal = centered * inv_std
    return (normal * gain_row + shift_row, normal, inv_std)


def norm_backward(grad_norm, normal, inv_std, gain_row):
    scaled = grad_norm * gain_row
    inner = (
        scaled
        - jnp.mean(scaled, axis=-1, keepdims=True)
        - normal * jnp.mean(scaled * normal, axis=-1, keepdims=True)
    )
    return inner * inv_std


def gelu_tanh(values):
    return jax.nn.gelu(values, approximate=True)


def gelu_back(values, grads):
    unused, pullback = jax.vjp(gelu_tanh, values)
    return pullback(grads)[0]


def pick_tree(flag, first_tree, second_tree):
    return jax.tree.map(partial(jnp.where, flag), first_tree, second_tree)


def gather_rows(values):
    return lax.all_gather(values, "tensor", axis=0, tiled=True)


def sum_rows(values):
    return lax.psum_scatter(
        values.astype(jnp.bfloat16), "tensor", scatter_dimension=0, tiled=True
    ).astype(jnp.float32)


def gather_grads(values):
    return lax.all_gather(values, "tensor", axis=0, tiled=True)


def sum_grads(values):
    return lax.psum_scatter(
        values.astype(jnp.bfloat16), "tensor", scatter_dimension=0, tiled=True
    ).astype(jnp.float32)


def fetch_weights(w_qkv, w_out, w_fc, w_proj):
    return (
        lax.all_gather(w_qkv[0], "dp", axis=0, tiled=True),
        lax.all_gather(w_out[0], "dp", axis=1, tiled=True),
        lax.all_gather(w_fc[0], "dp", axis=0, tiled=True),
        lax.all_gather(w_proj[0], "dp", axis=1, tiled=True),
    )


def scatter_grads(matrices):
    grad_qkv, grad_outproj, grad_fcin, grad_projout = matrices
    return (
        lax.psum_scatter(
            grad_qkv.astype(jnp.bfloat16), "dp", scatter_dimension=0, tiled=True
        ).astype(jnp.float32),
        lax.psum_scatter(
            grad_outproj.astype(jnp.bfloat16), "dp", scatter_dimension=1, tiled=True
        ).astype(jnp.float32),
        lax.psum_scatter(
            grad_fcin.astype(jnp.bfloat16), "dp", scatter_dimension=0, tiled=True
        ).astype(jnp.float32),
        lax.psum_scatter(
            grad_projout.astype(jnp.bfloat16), "dp", scatter_dimension=1, tiled=True
        ).astype(jnp.float32),
    )


def block_view(values, block_count, block_rows):
    return values.reshape((block_count, block_rows) + values.shape[1:])


def attend(queries, key_heads, value_heads, labels, block_rows):
    row_count = queries.shape[0]
    block_count = row_count // block_rows
    places = jnp.arange(row_count, dtype=jnp.int32)
    factor = queries.shape[-1] ** (-0.5)

    def one_block(pieces):
        query_block, label_block, place_block = pieces
        scores = (
            jnp.einsum("qhe,khe->hqk", query_block, key_heads, preferred_element_type=jnp.float32)
            * factor
        )
        visible = allowed(label_block, labels, place_block, places)
        scores = jnp.where(visible[None], scores, -1e30)
        highest = jnp.max(scores, axis=-1, keepdims=True)
        log_total = highest + jnp.log(jnp.sum(jnp.exp(scores - highest), axis=-1, keepdims=True))
        weights_low = jnp.exp(scores - log_total).astype(jnp.bfloat16)
        output = jnp.einsum(
            "hqk,khe->qhe", weights_low, value_heads, preferred_element_type=jnp.float32
        )
        return (output.astype(jnp.bfloat16), log_total[..., 0])

    pieces = (
        block_view(queries, block_count, block_rows),
        block_view(labels, block_count, block_rows),
        block_view(places, block_count, block_rows),
    )
    outputs, log_totals = lax.map(one_block, pieces)
    return (outputs.reshape(row_count, -1), log_totals)


def attend_back(queries, key_heads, value_heads, labels, log_totals, grad_output, block_rows):
    row_count, head_count, head_size = queries.shape
    block_count = row_count // block_rows
    places = jnp.arange(row_count, dtype=jnp.int32)
    factor = head_size ** (-0.5)

    def one_block(carry, pieces):
        grad_keys, grad_values = carry
        query_block, label_block, place_block, log_block, grad_block = pieces
        scores = (
            jnp.einsum("qhe,khe->hqk", query_block, key_heads, preferred_element_type=jnp.float32)
            * factor
        )
        visible = allowed(label_block, labels, place_block, places)
        scores = jnp.where(visible[None], scores, -1e30)
        weights_full = jnp.exp(scores - log_block[..., None])
        grad_values = grad_values + jnp.einsum(
            "hqk,qhe->khe",
            weights_full.astype(jnp.bfloat16),
            grad_block,
            preferred_element_type=jnp.float32,
        )
        grad_weights = jnp.einsum(
            "qhe,khe->hqk", grad_block, value_heads, preferred_element_type=jnp.float32
        )
        inner = jnp.sum(weights_full * grad_weights, axis=-1, keepdims=True)
        grad_scores = (weights_full * (grad_weights - inner)).astype(jnp.bfloat16)
        grad_query = (
            jnp.einsum("hqk,khe->qhe", grad_scores, key_heads, preferred_element_type=jnp.float32)
            * factor
        )
        grad_keys = (
            grad_keys
            + jnp.einsum(
                "hqk,qhe->khe", grad_scores, query_block, preferred_element_type=jnp.float32
            )
            * factor
        )
        return ((grad_keys, grad_values), grad_query)

    pieces = (
        block_view(queries, block_count, block_rows),
        block_view(labels, block_count, block_rows),
        block_view(places, block_count, block_rows),
        log_totals,
        block_view(grad_output, block_count, block_rows),
    )
    empty = jnp.zeros((row_count, head_count, head_size), jnp.float32)
    (grad_keys, grad_values), grad_queries = lax.scan(one_block, (empty, empty), pieces)
    return (grad_queries.reshape(row_count, head_count, head_size), grad_keys, grad_values)


def layer_forward(
    layer_input, current, gains, shifts, bias_qkv, bias_fc, labels_now, tensor_now, block_rows
):
    w_qkv_all, w_out_all, w_fc_all, w_proj_all = current
    local_rows = layer_input.shape[0]
    normed_first, normal_first, inv_first = norm_forward(layer_input, gains[0], shifts[0])
    gathered_first = gather_rows(normed_first.astype(jnp.bfloat16))
    row_count = gathered_first.shape[0]
    projected = (
        jnp.einsum("rd,dcf->rcf", gathered_first, w_qkv_all, preferred_element_type=jnp.float32)
        + bias_qkv[None]
    )
    projected = projected.astype(jnp.bfloat16)
    queries = projected[:, 0].reshape(row_count, -1, HD)
    key_heads = projected[:, 1].reshape(row_count, -1, HD)
    value_heads = projected[:, 2].reshape(row_count, -1, HD)
    attended, log_totals = attend(queries, key_heads, value_heads, labels_now, block_rows)
    hidden = (
        layer_input
        + sum_rows(jnp.dot(attended, w_out_all, preferred_element_type=jnp.float32))
        + shifts[2]
    )
    normed_second, normal_second, inv_second = norm_forward(hidden, gains[1], shifts[1])
    gathered_second = gather_rows(normed_second.astype(jnp.bfloat16))
    gelu_input = jnp.dot(gathered_second, w_fc_all, preferred_element_type=jnp.float32) + bias_fc
    activated = gelu_tanh(gelu_input).astype(jnp.bfloat16)
    valid_local = (
        lax.dynamic_slice_in_dim(labels_now, tensor_now * local_rows, local_rows) >= 0
    ).astype(jnp.float32)
    result = (
        hidden
        + sum_rows(jnp.dot(activated, w_proj_all, preferred_element_type=jnp.float32))
        + shifts[3]
    ) * valid_local[:, None]
    kept = (
        normal_first,
        inv_first,
        gathered_first,
        projected,
        attended,
        log_totals,
        normal_second,
        inv_second,
        gathered_second,
        gelu_input,
        activated,
        labels_now,
        valid_local,
    )
    return (result, kept)


def layer_backward(grad_input, current, gains, kept, block_rows):
    w_qkv_all, w_out_all, w_fc_all, w_proj_all = current
    (
        normal_first,
        inv_first,
        gathered_first,
        projected,
        attended,
        log_totals,
        normal_second,
        inv_second,
        gathered_second,
        gelu_input,
        activated,
        labels_now,
        valid_local,
    ) = kept
    row_count = gathered_first.shape[0]
    grad_out = grad_input * valid_local[:, None]
    grad_act_rows = gather_grads(grad_out.astype(jnp.bfloat16))
    grad_act = jnp.einsum(
        "rd,fd->rf", grad_act_rows, w_proj_all, preferred_element_type=jnp.float32
    )
    grad_gelu = gelu_back(gelu_input, grad_act).astype(jnp.bfloat16)
    grad_normed_second = sum_grads(
        jnp.einsum("rf,df->rd", grad_gelu, w_fc_all, preferred_element_type=jnp.float32)
    )
    grad_hidden = grad_out + norm_backward(grad_normed_second, normal_second, inv_second, gains[1])
    grad_mixed_rows = gather_grads(grad_hidden.astype(jnp.bfloat16))
    grad_attended = jnp.einsum(
        "rd,fd->rf", grad_mixed_rows, w_out_all, preferred_element_type=jnp.float32
    ).astype(jnp.bfloat16)
    queries = projected[:, 0].reshape(row_count, -1, HD)
    key_heads = projected[:, 1].reshape(row_count, -1, HD)
    value_heads = projected[:, 2].reshape(row_count, -1, HD)
    grad_queries, grad_keys, grad_values = attend_back(
        queries,
        key_heads,
        value_heads,
        labels_now,
        log_totals,
        grad_attended.reshape(row_count, -1, HD),
        block_rows,
    )
    grad_projected = (
        jnp.stack([grad_queries, grad_keys, grad_values], axis=1)
        .reshape(row_count, 3, -1)
        .astype(jnp.bfloat16)
    )
    grad_normed_first = sum_grads(
        jnp.einsum("rcf,dcf->rd", grad_projected, w_qkv_all, preferred_element_type=jnp.float32)
    )
    grad_result = grad_hidden + norm_backward(grad_normed_first, normal_first, inv_first, gains[0])
    saved = (
        grad_out,
        grad_act_rows,
        grad_gelu,
        grad_hidden,
        grad_mixed_rows,
        grad_projected,
        grad_normed_first,
        grad_normed_second,
    )
    return (grad_result, saved)


def weight_terms(kept, saved):
    (
        normal_first,
        inv_first,
        gathered_first,
        projected,
        attended,
        log_totals,
        normal_second,
        inv_second,
        gathered_second,
        gelu_input,
        activated,
        labels_now,
        valid_local,
    ) = kept
    (
        grad_out,
        grad_act_rows,
        grad_gelu,
        grad_hidden,
        grad_mixed_rows,
        grad_projected,
        grad_normed_first,
        grad_normed_second,
    ) = saved
    matrices = (
        jnp.einsum(
            "rd,rcf->dcf", gathered_first, grad_projected, preferred_element_type=jnp.float32
        ),
        jnp.einsum("rf,rd->fd", attended, grad_mixed_rows, preferred_element_type=jnp.float32),
        jnp.einsum("rd,rf->df", gathered_second, grad_gelu, preferred_element_type=jnp.float32),
        jnp.einsum("rf,rd->fd", activated, grad_act_rows, preferred_element_type=jnp.float32),
    )
    norm_term = jnp.stack(
        [
            jnp.sum(grad_normed_first * normal_first, axis=0),
            jnp.sum(grad_normed_second * normal_second, axis=0),
            jnp.sum(grad_normed_first, axis=0),
            jnp.sum(grad_normed_second, axis=0),
            jnp.sum(grad_hidden, axis=0),
            jnp.sum(grad_out, axis=0),
        ]
    )
    smalls = (
        jnp.sum(grad_projected, axis=0, dtype=jnp.float32),
        jnp.sum(grad_gelu, axis=0, dtype=jnp.float32),
        norm_term,
    )
    return (matrices, smalls)


def per_device(
    inputs,
    cotangent,
    w_qkv,
    b_qkv,
    w_out,
    w_fc,
    b_fc,
    w_proj,
    norm_gains,
    norm_shifts,
    seq_lengths,
    seq_ranks,
    seq_micros,
):
    section_now = lax.axis_index("section")
    rank_now = lax.axis_index("dp")
    tensor_now = lax.axis_index("tensor")
    micro_count = inputs.shape[0]
    local_rows = inputs.shape[1]
    width = inputs.shape[2]
    slot_rows = local_rows * lax.axis_size("tensor")
    block_rows = min(512, slot_rows)
    gains = norm_gains[0]
    shifts = norm_shifts[0]
    bias_qkv = b_qkv[0]
    bias_fc = b_fc[0]
    first_section = section_now == 0
    last_section = section_now == 1
    labels_all = [
        slot_labels(seq_lengths, seq_ranks, seq_micros, rank_now, micro_idx, slot_rows)
        for micro_idx in range(micro_count)
    ]
    forward_kept = []
    forward_out = []
    arriving = jnp.zeros((local_rows, width), jnp.bfloat16)
    for tick_now in range(micro_count + 1):
        own_micro = min(tick_now, micro_count - 1)
        prev_micro = max(tick_now - 1, 0)
        layer_input = jnp.where(first_section, inputs[own_micro], arriving).astype(jnp.float32)
        labels_now = jnp.where(first_section, labels_all[own_micro], labels_all[prev_micro])
        current = fetch_weights(w_qkv, w_out, w_fc, w_proj)
        result, kept = layer_forward(
            layer_input,
            current,
            gains,
            shifts,
            bias_qkv,
            bias_fc,
            labels_now,
            tensor_now,
            block_rows,
        )
        outgoing = result.astype(jnp.bfloat16)
        forward_kept.append(kept)
        forward_out.append(outgoing)
        if tick_now < micro_count:
            arriving = passed_along(outgoing, "section", 1)
    back_saved = []
    back_out = []
    returning = jnp.zeros((local_rows, width), jnp.bfloat16)
    for tick_now in range(micro_count + 1):
        own_micro = min(tick_now, micro_count - 1)
        kept = pick_tree(
            last_section,
            forward_kept[min(tick_now + 1, micro_count)],
            forward_kept[max(tick_now - 1, 0)],
        )
        grad_input = jnp.where(last_section, cotangent[own_micro], returning).astype(jnp.float32)
        current = fetch_weights(w_qkv, w_out, w_fc, w_proj)
        grad_result, saved = layer_backward(grad_input, current, gains, kept, block_rows)
        outgoing = grad_result.astype(jnp.bfloat16)
        back_saved.append(saved)
        back_out.append(outgoing)
        if tick_now < micro_count:
            returning = passed_along(outgoing, "section", -1)
    act_list = []
    grad_list = []
    matrix_sum = None
    small_sum = None
    for micro_idx in range(micro_count):
        act_list.append(jnp.where(last_section, forward_out[micro_idx + 1], forward_out[micro_idx]))
        grad_list.append(jnp.where(last_section, back_out[micro_idx], back_out[micro_idx + 1]))
        kept = pick_tree(last_section, forward_kept[micro_idx + 1], forward_kept[micro_idx])
        saved = pick_tree(last_section, back_saved[micro_idx], back_saved[micro_idx + 1])
        matrices, smalls = weight_terms(kept, saved)
        matrix_sum = matrices if matrix_sum is None else jax.tree.map(jnp.add, matrix_sum, matrices)
        small_sum = smalls if small_sum is None else jax.tree.map(jnp.add, small_sum, smalls)
    matrix_sum = scatter_grads(matrix_sum)
    norm_total = lax.psum(small_sum[2], "tensor")
    bias_qkv_grad, bias_fc_grad, norm_total = lax.psum(
        (small_sum[0], small_sum[1], norm_total), "dp"
    )
    activations = jnp.stack(act_list)[None]
    input_grads = jnp.stack(grad_list)[None]
    return (
        activations,
        input_grads,
        matrix_sum[0][None],
        bias_qkv_grad[None],
        matrix_sum[1][None],
        matrix_sum[2][None],
        bias_fc_grad[None],
        matrix_sum[3][None],
        norm_total[:2][None],
        norm_total[2:][None],
    )


def solution(mesh):
    placed = (
        P(None, ("dp", "tensor"), None),
        P(None, ("dp", "tensor"), None),
        P("section", "dp", None, "tensor"),
        P("section", None, "tensor"),
        P("section", "tensor", "dp"),
        P("section", "dp", "tensor"),
        P("section", "tensor"),
        P("section", "tensor", "dp"),
        P("section", None, None),
        P("section", None, None),
        P(),
        P(),
        P(),
    )
    return jax.shard_map(
        per_device,
        mesh=mesh,
        in_specs=placed,
        out_specs=(
            P("section", None, ("dp", "tensor"), None),
            P("section", None, ("dp", "tensor"), None),
            P("section", "dp", None, "tensor"),
            P("section", None, "tensor"),
            P("section", "tensor", "dp"),
            P("section", "dp", "tensor"),
            P("section", "tensor"),
            P("section", "tensor", "dp"),
            P("section", None, None),
            P("section", None, None),
        ),
        check_vma=False,
    )
```

profile of v0, /device:TPU:0, one launch (start us, length us, event | category | flops | bytes accessed | tf_op | source)
XLA Modules:
  0.0 894.0 jit_solution(4443685354549788293)
XLA Ops:
  10.0 25.9 %all-gather.1 = bf16[1,256,1024]{1,2,0:T(8,128)(2,1)S(1)} all-gather(bf16[1,256,64]{1,2,0:T(8,128)(2,1)} %param.17), channel_id=3, replica_groups=mesh['section'=2,'dp'=16,'tensor'=4] {'dp'}, dimensions={2}, use_global_device_ids=true | all-gather | bytes 557056 | tf_op jit(solution)/shard_map/all_gather | solution.py:91
  41.6 13.2 %all_gather.32 = bf16[256,1024]{1,0:T(8,128)(2,1)S(1)} all-gather(bf16[64,1024]{1,0:T(8,128)(2,1)S(1)} %fusion.247), channel_id=1, replica_groups=mesh['section'=2,'dp'=16,'tensor'=4] {'tensor'}, dimensions={0}, use_global_device_ids=true | all-gather | bytes 655360 | tf_op jit(solution)/shard_map/all_gather | solution.py:69
  62.6 19.4 %reduce-scatter.17.cloned.1.call-done = bf16[64,1024]{1,0:T(8,128)(2,1)} async-done(((bf16[256,1024]{1,0:T(8,128)(2,1)}), bf16[64,1024]{1,0:T(8,128)(2,1)}) %reduce-scatter.17.cloned.1.call-update) | async-done | bytes 131088 | tf_op jit(solution)/shard_map/reduce_scatter | solution.py:73
  85.3 12.8 %all_gather.35 = bf16[256,1024]{1,0:T(8,128)(2,1)S(1)} all-gather(bf16[64,1024]{1,0:T(8,128)(2,1)S(1)} %add_convert_fusion.5), channel_id=1, replica_groups=mesh['section'=2,'dp'=16,'tensor'=4] {'tensor'}, dimensions={0}, use_global_device_ids=true | all-gather | bytes 655360 | tf_op jit(solution)/shard_map/all_gather | solution.py:69
  98.1 31.2 %all-gather.10.cloned.1.call-done = bf16[1,1024,1024]{2,1,0:T(8,128)(2,1)} async-done(((bf16[1,64,1024]{2,1,0:T(8,128)(2,1)}), bf16[1,1024,1024]{2,1,0:T(8,128)(2,1)}) %all-gather.10.cloned.1.call-update) | async-done | bytes 2097168 | tf_op jit(solution)/shard_map/all_gather | solution.py:92
  131.6 44.2 %all-gather.12.cloned.1.call-done = bf16[1,1024,1024]{1,2,0:T(8,128)(2,1)} async-done(((bf16[1,1024,64]{1,2,0:T(8,128)(2,1)}), bf16[1,1024,1024]{1,2,0:T(8,128)(2,1)}) %all-gather.12.cloned.1.call-update) | async-done | bytes 2097168 | tf_op jit(solution)/shard_map/all_gather | solution.py:93
  181.0 18.9 %reduce-scatter.19.cloned.1.call-done = bf16[64,1024]{1,0:T(8,128)(2,1)} async-done(((bf16[256,1024]{1,0:T(8,128)(2,1)}), bf16[64,1024]{1,0:T(8,128)(2,1)}) %reduce-scatter.19.cloned.1.call-update) | async-done | bytes 131088 | tf_op jit(solution)/shard_map/reduce_scatter | solution.py:73
  203.8 13.5 %all_gather.74 = bf16[256,1024]{1,0:T(8,128)(2,1)S(1)} all-gather(bf16[64,1024]{1,0:T(8,128)(2,1)S(1)} %fusion.244), channel_id=1, replica_groups=mesh['section'=2,'dp'=16,'tensor'=4] {'tensor'}, dimensions={0}, use_global_device_ids=true | all-gather | bytes 655360 | tf_op jit(solution)/shard_map/all_gather | solution.py:69
  221.7 21.2 %reduce-scatter.21.cloned.1.call-done = bf16[64,1024]{1,0:T(8,128)(2,1)} async-done(((bf16[256,1024]{1,0:T(8,128)(2,1)}), bf16[64,1024]{1,0:T(8,128)(2,1)}) %reduce-scatter.21.cloned.1.call-update) | async-done | bytes 131088 | tf_op jit(solution)/shard_map/reduce_scatter | solution.py:73
  263.3 13.5 %all_gather.78 = bf16[256,1024]{1,0:T(8,128)(2,1)S(1)} all-gather(bf16[64,1024]{1,0:T(8,128)(2,1)S(1)} %fusion.280), channel_id=1, replica_groups=mesh['section'=2,'dp'=16,'tensor'=4] {'tensor'}, dimensions={0}, use_global_device_ids=true | all-gather | bytes 655360 | tf_op jit(solution)/shard_map/all_gather | solution.py:79
  288.5 19.9 %reduce-scatter.29.cloned.1.call-done = bf16[64,1024]{1,0:T(8,128)(2,1)} async-done(((bf16[256,1024]{1,0:T(8,128)(2,1)}), bf16[64,1024]{1,0:T(8,128)(2,1)}) %reduce-scatter.29.cloned.1.call-update) | async-done | bytes 131088 | tf_op jit(solution)/shard_map/reduce_scatter | solution.py:83
  334.4 17.2 %reduce-scatter.25.cloned.1.call-done = bf16[64,1024]{1,0:T(8,128)(2,1)} async-done(((bf16[256,1024]{1,0:T(8,128)(2,1)}), bf16[64,1024]{1,0:T(8,128)(2,1)}) %reduce-scatter.25.cloned.1.call-update) | async-done | bytes 131088 | tf_op jit(solution)/shard_map/reduce_scatter | solution.py:73
  373.7 13.7 %all_gather.77 = bf16[256,1024]{1,0:T(8,128)(2,1)} all-gather(bf16[64,1024]{1,0:T(8,128)(2,1)} %get-tuple-element.324), channel_id=1, replica_groups=mesh['section'=2,'dp'=16,'tensor'=4] {'tensor'}, dimensions={0}, use_global_device_ids=true | all-gather | bytes 655360 | tf_op jit(solution)/shard_map/all_gather | solution.py:69
  401.3 13.3 %all_gather.80 = bf16[256,1024]{1,0:T(8,128)(2,1)S(1)} all-gather(bf16[64,1024]{1,0:T(8,128)(2,1)S(1)} %get-tuple-element.259), channel_id=1, replica_groups=mesh['section'=2,'dp'=16,'tensor'=4] {'tensor'}, dimensions={0}, use_global_device_ids=true | all-gather | bytes 655360 | tf_op jit(solution)/shard_map/all_gather | solution.py:79
  422.2 18.2 %reduce-scatter.33.cloned.1.call-done = bf16[64,1024]{1,0:T(8,128)(2,1)} async-done(((bf16[256,1024]{1,0:T(8,128)(2,1)}), bf16[64,1024]{1,0:T(8,128)(2,1)}) %reduce-scatter.33.cloned.1.call-update) | async-done | bytes 131088 | tf_op jit(solution)/shard_map/reduce_scatter | solution.py:83
  461.1 21.0 %reduce-scatter.35.cloned.1.call-done = bf16[64,1024]{1,0:T(8,128)(2,1)} async-done(((bf16[256,1024]{1,0:T(8,128)(2,1)}), bf16[64,1024]{1,0:T(8,128)(2,1)}) %reduce-scatter.35.cloned.1.call-update) | async-done | bytes 131088 | tf_op jit(solution)/shard_map/reduce_scatter | solution.py:83
  491.7 13.4 %all_gather.82 = bf16[256,1024]{1,0:T(8,128)(2,1)S(1)} all-gather(bf16[64,1024]{1,0:T(8,128)(2,1)S(1)} %fusion.282), channel_id=1, replica_groups=mesh['section'=2,'dp'=16,'tensor'=4] {'tensor'}, dimensions={0}, use_global_device_ids=true | all-gather | bytes 655360 | tf_op jit(solution)/shard_map/all_gather | solution.py:79
  517.1 15.8 %reduce-scatter.37.cloned.1.call-done = bf16[64,1024]{1,0:T(8,128)(2,1)} async-done(((bf16[256,1024]{1,0:T(8,128)(2,1)}), bf16[64,1024]{1,0:T(8,128)(2,1)}) %reduce-scatter.37.cloned.1.call-update) | async-done | bytes 131088 | tf_op jit(solution)/shard_map/reduce_scatter | solution.py:83
  536.6 14.0 %all_gather.83 = bf16[256,1024]{1,0:T(8,128)(2,1)S(1)} all-gather(bf16[64,1024]{1,0:T(8,128)(2,1)S(1)} %convert_element_type.356), channel_id=1, replica_groups=mesh['section'=2,'dp'=16,'tensor'=4] {'tensor'}, dimensions={0}, use_global_device_ids=true | all-gather | bytes 655360 | tf_op jit(solution)/shard_map/all_gather | solution.py:79
  580.9 15.0 %psum.30 = f32[6,1024]{1,0:T(8,128)S(1)} all-reduce(f32[6,1024]{1,0:T(8,128)S(1)} %add.616), channel_id=1, replica_groups=mesh['section'=2,'dp'=16,'tensor'=4] {'tensor'}, use_global_device_ids=true, to_apply=%region_71.72 | all-reduce | flops 6144 | bytes 49152 | tf_op jit(solution)/shard_map/psum | solution.py:461
  595.9 75.1 %all-reduce = (f32[1,3,256]{2,0,1:T(1,128)}, f32[1,1024]{1,0:T(1,128)}, f32[6,1024]{1,0:T(8,128)S(1)}) all-reduce(f32[1,3,256]{2,0,1:T(1,128)S(1)} %broadcast_in_dim.305, f32[1,1024]{1,0:T(1,128)S(1)} %bitcast.477, f32[6,1024]{1,0:T(8,128)S(1)} %psum.30), channel_id=1, replica_groups=mesh['section'=2,'dp'=16,'tensor'=4] {'dp'}, use_global_device_ids=true, to_apply=%region_52.53 | all-reduce | flops 7936 | bytes 63488 | tf_op jit(solution)/shard_map/psum | solution.py:462
  675.6 55.8 %reduce-scatter.41.cloned.1.call-done = bf16[64,3,256]{2,0,1:T(8,128)(2,1)} async-done(((bf16[1024,3,256]{2,0,1:T(8,128)(2,1)}), bf16[64,3,256]{2,0,1:T(8,128)(2,1)}) %reduce-scatter.41.cloned.1.call-update) | async-done | bytes 98320 | tf_op jit(solution)/shard_map/reduce_scatter | solution.py:100
  732.9 75.5 %reduce-scatter.45.cloned.1.call-done = bf16[64,1024]{1,0:T(8,128)(2,1)} async-done(((bf16[1024,1024]{1,0:T(8,128)(2,1)}), bf16[64,1024]{1,0:T(8,128)(2,1)}) %reduce-scatter.45.cloned.1.call-update) | async-done | bytes 131088 | tf_op jit(solution)/shard_map/reduce_scatter | solution.py:106
  810.0 75.4 %reduce-scatter.47.cloned.1.call-done = bf16[1024,64]{0,1:T(8,128)(2,1)} async-done(((bf16[1024,1024]{0,1:T(8,128)(2,1)}), bf16[1024,64]{0,1:T(8,128)(2,1)}) %reduce-scatter.47.cloned.1.call-update) | async-done | bytes 131088 | tf_op jit(solution)/shard_map/reduce_scatter | solution.py:109
  (533 shorter events, 220.4 us)
Async XLA Ops:
  7.2 49.7 %all-gather.8.cloned.1.call-start = ((), (), s32[]{:S(2)}) async-start(), calls=%async_computation.32 | async-start | bytes 1671168 | tf_op jit(solution)/shard_map/all_gather | solution.py:90
  7.9 74.1 %reduce-scatter.17.cloned.1.call-start = ((), (), s32[]{:S(2)}) async-start(), calls=%async_computation.16 | async-start | bytes 655360 | tf_op jit(solution)/shard_map/reduce_scatter | solution.py:73
  40.5 244.2 %copy-start.93 = (f32[1,1,1024]{2,1,0:T(1,128)}, f32[1,1,1024]{2,1,0:T(1,128)S(1)}, u32[]{:S(2)}) copy-start(f32[1,1,1024]{2,1,0:T(1,128)S(1)} %get-tuple-element.318) | copy-start | bytes 12292
  61.3 68.0 %all-gather.10.cloned.1.call-start = ((), (), s32[]{:S(2)}) async-start(), calls=%async_computation.33 | async-start | bytes 2228224 | tf_op jit(solution)/shard_map/all_gather | solution.py:92
  62.0 113.8 %all-gather.12.cloned.1.call-start = ((), (), s32[]{:S(2)}) async-start(), calls=%async_computation.34 | async-start | bytes 2228224 | tf_op jit(solution)/shard_map/all_gather | solution.py:93
  62.6 137.3 %reduce-scatter.19.cloned.1.call-start = ((), (), s32[]{:S(2)}) async-start(), calls=%async_computation.17 | async-start | bytes 655360 | tf_op jit(solution)/shard_map/reduce_scatter | solution.py:73
  179.1 63.7 %reduce-scatter.21.cloned.1.call-start = ((), (), s32[]{:S(2)}) async-start(), calls=%async_computation.18 | async-start | bytes 655360 | tf_op jit(solution)/shard_map/reduce_scatter | solution.py:73
  201.0 2.3 collective-permute-start
  221.6 63.2 %reduce-scatter.23.cloned.1.call-start = ((), (), s32[]{:S(2)}) async-start(), calls=%async_computation.19 | async-start | bytes 655360 | tf_op jit(solution)/shard_map/reduce_scatter | solution.py:73
  263.1 45.3 %reduce-scatter.29.cloned.1.call-start = ((), (), s32[]{:S(2)}) async-start(), calls=%async_computation.22 | async-start | bytes 655360 | tf_op jit(solution)/shard_map/reduce_scatter | solution.py:83
  283.3 68.2 %reduce-scatter.25.cloned.1.call-start = ((), (), s32[]{:S(2)}) async-start(), calls=%async_computation.20 | async-start | bytes 655360 | tf_op jit(solution)/shard_map/reduce_scatter | solution.py:73
  286.4 22.0 %collective-permute-start.1 = (bf16[64,1024]{1,0:T(8,128)(2,1)S(1)}, bf16[64,1024]{1,0:T(8,128)(2,1)S(1)}, u32[]{:S(2)}, u32[]{:S(2)}) collective-permute-start(bf16[64,1024]{1,0:T(8,128)(2,1)S(1)} %get-tuple-element.284), channel_id=1, source_target_pairs={{0,64},{1,65},{2,66},{3,67},{4,68},{5,69},{6,70},{7,71},{8,72},{9,... | collective-permute-start | bytes 393224 | tf_op jit(solution)/shard_map/ppermute | solution.py:17
  330.3 64.5 %reduce-scatter.31.cloned.1.call-start = ((), (), s32[]{:S(2)}) async-start(), calls=%async_computation.23 | async-start | bytes 655360 | tf_op jit(solution)/shard_map/reduce_scatter | solution.py:83
  373.6 66.8 %reduce-scatter.33.cloned.1.call-start = ((), (), s32[]{:S(2)}) async-start(), calls=%async_computation.24 | async-start | bytes 655360 | tf_op jit(solution)/shard_map/reduce_scatter | solution.py:83
  397.2 4.0 collective-permute-start.2
  419.1 63.0 %reduce-scatter.35.cloned.1.call-start = ((), (), s32[]{:S(2)}) async-start(), calls=%async_computation.25 | async-start | bytes 655360 | tf_op jit(solution)/shard_map/reduce_scatter | solution.py:83
  460.8 72.0 %reduce-scatter.37.cloned.1.call-start = ((), (), s32[]{:S(2)}) async-start(), calls=%async_computation.26 | async-start | bytes 655360 | tf_op jit(solution)/shard_map/reduce_scatter | solution.py:83
  485.9 3.2 collective-permute-start.3
  511.5 63.6 %reduce-scatter.27.cloned.1.call-start = ((), (), s32[]{:S(2)}) async-start(), calls=%async_computation.21 | async-start | bytes 655360 | tf_op jit(solution)/shard_map/reduce_scatter | solution.py:73
  517.0 62.6 %reduce-scatter.39.cloned.1.call-start = ((), (), s32[]{:S(2)}) async-start(), calls=%async_computation.27 | async-start | bytes 655360 | tf_op jit(solution)/shard_map/reduce_scatter | solution.py:83
  555.0 119.2 %reduce-scatter.43.cloned.1.call-start = ((), (), s32[]{:S(2)}) async-start(), calls=%async_computation.29 | async-start | bytes 557056 | tf_op jit(solution)/shard_map/reduce_scatter | solution.py:103
  558.3 173.0 %reduce-scatter.41.cloned.1.call-start = ((), (), s32[]{:S(2)}) async-start(), calls=%async_computation.28 | async-start | bytes 1671168 | tf_op jit(solution)/shard_map/reduce_scatter | solution.py:100
  563.0 245.4 %reduce-scatter.45.cloned.1.call-start = ((), (), s32[]{:S(2)}) async-start(), calls=%async_computation.30 | async-start | bytes 2228224 | tf_op jit(solution)/shard_map/reduce_scatter | solution.py:106
  568.1 317.4 %reduce-scatter.47.cloned.1.call-start = ((), (), s32[]{:S(2)}) async-start(), calls=%async_computation.31 | async-start | bytes 2228224 | tf_op jit(solution)/shard_map/reduce_scatter | solution.py:109
  (154 other events, 2844.6 us)
Sparse Core Ops, SparseCore 0:
  10.2 46.6 all-gather.7
  61.4 20.6 reduce-scatter.16
  84.2 45.0 all-gather.9
  131.3 44.5 all-gather.11
  179.3 20.5 reduce-scatter.18
  221.7 21.1 reduce-scatter.20
  263.2 21.4 reduce-scatter.22
  287.1 21.2 reduce-scatter.28
  330.4 21.0 reduce-scatter.24
  373.7 20.9 reduce-scatter.30
  419.3 21.0 reduce-scatter.32
  461.0 21.1 reduce-scatter.34
  511.6 21.1 reduce-scatter.36
  535.1 21.0 reduce-scatter.26
  558.4 21.1 reduce-scatter.38
  582.6 72.1 reduce-scatter.42
  658.3 73.0 reduce-scatter.40
  734.8 73.5 reduce-scatter.44
  811.7 73.7 reduce-scatter.46
where the time goes:
time: 904 us; the launch traced here: 894 us
  waiting for transfers between devices  450 us (50%)
  blocking collectives  275 us (30%)
  matrix products  65.4 us (7%)
  other arithmetic  60.8 us (7%)
  local copies, waits for them, and re-layouts  20.1 us (2%)
  between operations  16.4 us (2%)
    reduce_scatter x6, waiting for transfers between devices, sum_grads(): lax.psum_scatter(values.astype(jnp.bfloat16), 'tensor', scatter_dimension...  84.2 us
    all_gather x6, blocking collectives, gather_grads(): return lax.all_gather(values, 'tensor', axis=0, tiled=True)  79.9 us
    all_gather x6, blocking collectives, gather_rows(): return lax.all_gather(values, 'tensor', axis=0, tiled=True)  78.8 us
    reduce_scatter x6, waiting for transfers between devices, sum_rows(): lax.psum_scatter(values.astype(jnp.bfloat16), 'tensor', scatter_dimension...  77.9 us
    reduce_scatter x1, waiting for transfers between devices, scatter_grads(): lax.psum_scatter(grad_fcin.astype(jnp.bfloat16), 'dp', scatter_dimension=...  75.5 us
    reduce_scatter x1, waiting for transfers between devices, scatter_grads(): lax.psum_scatter(grad_projout.astype(jnp.bfloat16), 'dp', scatter_dimensi...  75.4 us
    psum x1, blocking collectives, per_device(): lax.psum((small_sum[0], small_sum[1], norm_total), 'dp')  75.1 us
    reduce_scatter x1, waiting for transfers between devices, scatter_grads(): lax.psum_scatter(grad_qkv.astype(jnp.bfloat16), 'dp', scatter_dimension=0...  55.8 us
  transfers between devices with their start and end apart: 23, of which 19 were waited for; matrix products, arithmetic and copies ran while one was open for 8% of the time, Pallas kernels for 0%

commit v1 on v0

v1 whole, which is shorter than its diff:
```python
import jax
import jax.numpy as jnp
from jax import lax
from jax.experimental import pallas as pl
from jax.experimental.pallas import tpu as pltpu
from jax.sharding import PartitionSpec as P

HD = 64
EPS = 1e-05
MESH = pl.DeviceIdType.MESH
F32 = jnp.float32
BF16 = jnp.bfloat16
GELU_A = 0.7978845608028654
GELU_B = 0.044715


def nn(a, b):
    return lax.dot_general(a, b, (((1,), (0,)), ((), ())), preferred_element_type=F32)


def nt(a, b):
    return lax.dot_general(a, b, (((1,), (1,)), ((), ())), preferred_element_type=F32)


def tn(a, b):
    return lax.dot_general(a, b, (((0,), (0,)), ((), ())), preferred_element_type=F32)


def norm(values):
    average = jnp.mean(values, axis=-1, keepdims=True)
    centered = values - average
    inv = lax.rsqrt(jnp.mean(centered * centered, axis=-1, keepdims=True) + EPS)
    return centered * inv, inv


def norm_back(grad, normal, inv, gain):
    scaled = grad * gain
    return inv * (
        scaled
        - jnp.mean(scaled, axis=-1, keepdims=True)
        - normal * jnp.mean(scaled * normal, axis=-1, keepdims=True)
    )


def gelu(u):
    return 0.5 * u * (1.0 + jnp.tanh(GELU_A * (u + GELU_B * u * u * u)))


def gelu_slope(u):
    square = u * u
    t = jnp.tanh(GELU_A * u * (1.0 + GELU_B * square))
    return 0.5 * (1.0 + t) + 0.5 * u * (1.0 - t * t) * (GELU_A * (1.0 + 3.0 * GELU_B * square))


class Sizes:
    def __init__(self, z, y, t, rows, width, heads, hidden):
        self.Z, self.Y, self.T = z, y, t
        self.LR, self.D, self.E, self.F = rows, width, heads, hidden
        self.R = rows * t
        self.C = 2
        self.DC = width // self.C
        self.B = width // (z * y)
        self.HB = self.B // 2
        self.names = ("q", "o", "f", "p")
        self.width = {"q": 3 * heads, "o": heads, "f": hidden, "p": hidden}


def kernel_body(sz, n_sems, *refs):
    names = sz.names
    Z, Y, T, LR, D, E, F, R = sz.Z, sz.Y, sz.T, sz.LR, sz.D, sz.E, sz.F, sz.R
    C, DC, HB, B = sz.C, sz.DC, sz.HB, sz.B
    it = iter(refs)
    x_in, cot_in = next(it), next(it)
    shard = {m: next(it) for m in names}
    pack_in, seq_in = next(it), next(it)
    act_out, grad_out = next(it), next(it)
    gout = {m: next(it) for m in names}
    small_out = next(it)
    W = {m: next(it) for m in names}
    G = {m: next(it) for m in names}
    SIB = {m: next(it) for m in names}
    RA = {m: next(it) for m in names}
    RB = {m: next(it) for m in names}
    R2A = {m: next(it) for m in names}
    R2B = {m: next(it) for m in names}
    pack = next(it)
    A, Cn, DM, DH = next(it), next(it), next(it), next(it)
    QKV, O, PR, U, Gl = next(it), next(it), next(it), next(it), next(it)
    DU, DO, DQKV = next(it), next(it), next(it)
    N1, I1, N2, I2 = next(it), next(it), next(it), next(it)
    HID = next(it)
    MASK = next(it)
    stage, recv = next(it), next(it)
    small, small_sib, small_x, small_y, small_z = next(it), next(it), next(it), next(it), next(it)
    act_send, act_recv, ig_send, ig_recv = next(it), next(it), next(it), next(it)
    send_sem, recv_sem = next(it), next(it)

    s = lax.axis_index("section")
    d = lax.axis_index("dp")
    t = lax.axis_index("tensor")
    z = d // Y
    y = d % Y
    count = [0]
    drains = []

    def copy(src, dst, device, when=None):
        i = count[0]
        count[0] += 1
        c = pltpu.make_async_remote_copy(
            src_ref=src,
            dst_ref=dst,
            send_sem=send_sem.at[i],
            recv_sem=recv_sem.at[i],
            device_id=device,
            device_id_type=MESH,
        )
        drains.append((c, when))
        return c

    def at_x(k):
        return (s, d, (t + k) % T)

    def at_y(k):
        return (s, z * Y + (y + k) % Y, t)

    def at_z(k):
        return (s, ((z + k) % Z) * Y + y, t)

    sibling = (1 - s, d, t)

    def far_first(n):
        return sorted(range(1, n), key=lambda k: -min(k, n - k))

    barrier = pltpu.get_barrier_semaphore()
    peers = (
        [at_x(k) for k in range(1, T)]
        + [at_y(k) for k in range(1, Y)]
        + [at_z(k) for k in range(1, Z)]
        + [sibling]
    )
    for p in peers:
        pl.semaphore_signal(barrier, inc=1, device_id=p, device_id_type=MESH)

    for m in names:
        W[m][s, z, y] = shard[m][...]
    pack[s] = pack_in[...]
    pl.semaphore_wait(barrier, len(peers))

    pack_copy = copy(pack.at[s], pack.at[s], sibling)
    pack_copy.start()

    class Gather:
        def __init__(self, l, m):
            w = W[m]
            self.one_a = [
                copy(w.at[l, z, y, pl.ds(0, HB)], w.at[l, z, y, pl.ds(0, HB)], at_y(k), l)
                for k in far_first(Y)
            ]
            self.one_b = [
                copy(w.at[l, z, y, pl.ds(HB, HB)], w.at[l, z, y, pl.ds(HB, HB)], at_z(k), l)
                for k in far_first(Z)
            ]
            self.two_a = [
                copy(w.at[l, z, :, pl.ds(0, HB)], w.at[l, z, :, pl.ds(0, HB)], at_z(k), l)
                for k in far_first(Z)
            ]
            self.two_b = [
                copy(w.at[l, :, y, pl.ds(HB, HB)], w.at[l, :, y, pl.ds(HB, HB)], at_y(k), l)
                for k in far_first(Y)
            ]
            self.over = copy(w.at[l], w.at[l], sibling, l)

        def one(self):
            for c in self.one_a + self.one_b:
                c.start()

        def two(self):
            for c in self.one_a:
                c.wait_recv()
            for c in self.two_a:
                c.start()
            for c in self.one_b:
                c.wait_recv()
            for c in self.two_b:
                c.start()

        def three(self):
            for c in self.two_a + self.two_b:
                c.wait_recv()
            self.over.start()

        def arrive(self):
            self.over.wait_recv()

    gathers = [{m: Gather(l, m) for m in names} for l in range(2)]

    def on(core, f):
        pl.when(s == core)(f)

    def phase(l, step, *ms):
        def go():
            for m in ms:
                getattr(gathers[l][m], step)()

        on(l, go)

    def ready(l, m):
        on(l, gathers[l][m].three)
        on(1 - l, gathers[l][m].arrive)

    phase(0, "one", "q", "o", "f", "p")

    seqs = seq_in[...].astype(F32)
    n_seq = seqs.shape[1]
    lengths, ranks, micros = seqs[0:1], seqs[1:2], seqs[2:3]
    mine_row = jnp.logical_and(ranks == d.astype(F32), micros == s.astype(F32))
    taken_row = jnp.where(mine_row, lengths, 0.0)
    i0 = lax.broadcasted_iota(jnp.int32, (n_seq, n_seq), 0)
    i1 = lax.broadcasted_iota(jnp.int32, (n_seq, n_seq), 1)
    taken_col = jnp.sum(jnp.where(i0 == i1, taken_row, 0.0), axis=1, keepdims=True)
    ends_col = jnp.sum(jnp.where(i1 <= i0, taken_row, 0.0), axis=1, keepdims=True)
    ends_row = jnp.sum(jnp.where(i0 <= i1, taken_col, 0.0), axis=0, keepdims=True)
    number_row = lax.broadcasted_iota(jnp.int32, (1, n_seq), 1).astype(F32) + 1.0
    number_col = lax.broadcasted_iota(jnp.int32, (n_seq, 1), 0).astype(F32) + 1.0

    def column_labels(rows, first):
        places = (lax.broadcasted_iota(jnp.int32, (rows, n_seq), 0) + first).astype(F32)
        inside = jnp.logical_and(places >= ends_row - taken_row, places < ends_row)
        return jnp.sum(jnp.where(inside, number_row, 0.0), axis=1, keepdims=True)

    label_col = column_labels(R, 0)
    places = lax.broadcasted_iota(jnp.int32, (n_seq, R), 1).astype(F32)
    inside = jnp.logical_and(places >= ends_col - taken_col, places < ends_col)
    label_row = jnp.sum(jnp.where(inside, number_col, 0.0), axis=0, keepdims=True)
    r0 = lax.broadcasted_iota(jnp.int32, (R, R), 0)
    r1 = lax.broadcasted_iota(jnp.int32, (R, R), 1)
    same = jnp.logical_and(label_col == label_row, label_col > 0.5)
    visible = jnp.logical_or(jnp.logical_and(same, r1 <= r0), r0 == r1)
    MASK[...] = jnp.where(visible, 1.0, 0.0)
    valid = jnp.where(column_labels(LR, t * LR) > 0.5, 1.0, 0.0)

    pack_copy.wait_recv()

    def gain(l, i):
        return pack[l, i : i + 1, :]

    def shift(l, i):
        return pack[l, 2 + i : 3 + i, :]

    def gather_x(buf):
        copies = [copy(buf.at[t], buf.at[t], at_x(k)) for k in far_first(T)]
        for c in copies:
            c.start()

        def wait():
            for c in copies:
                c.wait_recv()

        return wait

    stage_busy = {}
    stage_turn = [0]

    def scatter_x(part):
        turn = stage_turn[0]
        stage_turn[0] += 1
        slot = turn % 2
        for c in stage_busy.get(slot, []):
            c.wait_send()
            drains[:] = [p for p in drains if p[0] is not c]
        copies = []
        for c in range(C):
            stage[slot, c] = part(c).astype(BF16).reshape(T, LR, DC)
            for k in far_first(T):
                one = copy(stage.at[slot, c, (t + k) % T], recv.at[turn, c, k - 1], at_x(k))
                one.start()
                copies.append(one)
        stage_busy[slot] = copies

        def total():
            for c in copies:
                c.wait_recv()
            out = []
            for c in range(C):
                v = stage[slot, c, t].astype(F32)
                for k in range(1, T):
                    v = v + recv[turn, c, k - 1].astype(F32)
                out.append(v)
            return jnp.concatenate(out, axis=1)

        return total

    lanes = lax.broadcasted_iota(jnp.int32, (R, 2 * HD), 1)

    def half(v, h):
        keep = lanes < HD if h == 0 else lanes >= HD
        return jnp.where(keep, v, jnp.zeros_like(v))

    factor = HD ** (-0.5)

    def rows_of(buf):
        return buf[...].reshape(R, D)

    def weight(m, l):
        return W[m][l].reshape(D, sz.width[m])

    def weight_rows(m, l, c):
        span = Z // C
        return W[m][l, c * span : (c + 1) * span].reshape(DC, sz.width[m])

    def layer_forward(l, X, at_a, at_b, at_c, at_d):
        n1, inv1 = norm(X)
        N1[l] = n1
        I1[l] = inv1
        A[l, t] = (n1 * gain(l, 0) + shift(l, 0)).astype(BF16)
        wait = gather_x(A.at[l])
        at_a()
        ready(l, "q")
        wait()
        bias = pack[l, 7:8, : 3 * E]
        QKV[l] = (nn(rows_of(A.at[l]), weight("q", l)) + bias).astype(BF16)
        for pair in range(E // (2 * HD)):
            lo = pair * 2 * HD
            q2 = QKV[l, :, lo : lo + 2 * HD]
            k2 = QKV[l, :, E + lo : E + lo + 2 * HD]
            v2 = QKV[l, :, 2 * E + lo : 2 * E + lo + 2 * HD]
            o2 = None
            for h in range(2):
                S = nt(q2, half(k2, h)) * factor
                S = jnp.where(MASK[...] > 0.5, S, -1e30)
                e = jnp.exp(S - jnp.max(S, axis=-1, keepdims=True))
                pr = (e / jnp.sum(e, axis=-1, keepdims=True)).astype(BF16)
                PR[l, pair * 2 + h] = pr
                part = nn(pr, half(v2, h))
                o2 = part if o2 is None else o2 + part
            O[l, :, lo : lo + 2 * HD] = o2.astype(BF16)
        ready(l, "o")
        total = scatter_x(lambda c: nt(O[l], weight_rows("o", l, c)))
        at_b()
        hidden = X + total() + shift(l, 2)
        n2, inv2 = norm(hidden)
        N2[l] = n2
        I2[l] = inv2
        HID[...] = hidden
        Cn[l, t] = (n2 * gain(l, 1) + shift(l, 1)).astype(BF16)
        wait = gather_x(Cn.at[l])
        at_c()
        ready(l, "f")
        wait()
        step = F // 2
        for j in range(2):
            cols = slice(j * step, (j + 1) * step)
            u = nn(rows_of(Cn.at[l]), W["f"][l, :, :, :, cols].reshape(D, step)) + pack[l, 6:7, cols]
            U[l, :, cols] = u
            Gl[l, :, cols] = gelu(u).astype(BF16)
        ready(l, "p")
        total = scatter_x(lambda c: nt(Gl[l], weight_rows("p", l, c)))
        at_d()
        return (HID[...] + total() + shift(l, 3)) * valid

    def grad_matrix(m, l, left, right):
        span = D // Z

        def step(i, carry):
            cols = pl.ds(pl.multiple_of(i * span, span), span)
            block = tn(left[:, :, cols].reshape(R, span), right())
            G[m][l, i] = block.astype(BF16).reshape(Y, B, sz.width[m])
            return carry

        lax.fori_loop(0, Z, step, 0)

    class Reduce:
        def __init__(self, l, m):
            self.l, self.m = l, m
            g = G[m]
            self.over = copy(g.at[l], SIB[m], sibling, 1 - l)
            self.one_a = [
                copy(g.at[l, :, (y + k) % Y, pl.ds(0, HB)], RA[m].at[k - 1], at_y(k), l)
                for k in far_first(Y)
            ]
            self.one_b = [
                copy(g.at[l, (z + k) % Z, :, pl.ds(HB, HB)], RB[m].at[k - 1], at_z(k), l)
                for k in far_first(Z)
            ]
            self.two_a = [
                copy(g.at[l, (z + k) % Z, y, pl.ds(0, HB)], R2A[m].at[k - 1], at_z(k), l)
                for k in far_first(Z)
            ]
            self.two_b = [
                copy(g.at[l, z, (y + k) % Y, pl.ds(HB, HB)], R2B[m].at[k - 1], at_y(k), l)
                for k in far_first(Y)
            ]

        def send(self):
            self.over.start()

        def add(self):
            g, l, m = G[self.m], self.l, self.m
            self.over.wait_recv()

            def step(i, carry):
                g[l, i] = (g[l, i].astype(F32) + SIB[m][i].astype(F32)).astype(BF16)
                return carry

            lax.fori_loop(0, Z, step, 0)
            for c in self.one_a + self.one_b:
                c.start()

        def middle(self):
            g, l, m = G[self.m], self.l, self.m
            for c in self.one_a:
                c.wait_recv()
            for i in range(Z):
                v = g[l, i, y, 0:HB].astype(F32)
                for k in range(Y - 1):
                    v = v + RA[m][k, i].astype(F32)
                g[l, i, y, 0:HB] = v.astype(BF16)
            for c in self.two_a:
                c.start()
            for c in self.one_b:
                c.wait_recv()
            for i in range(Y):
                v = g[l, z, i, HB:B].astype(F32)
                for k in range(Z - 1):
                    v = v + RB[m][k, i].astype(F32)
                g[l, z, i, HB:B] = v.astype(BF16)
            for c in self.two_b:
                c.start()

        def last(self):
            g, l, m = G[self.m], self.l, self.m
            for c in self.two_a + self.two_b:
                c.wait_recv()
            v = g[l, z, y, 0:HB].astype(F32)
            for k in range(Z - 1):
                v = v + R2A[m][k].astype(F32)
            gout[m][0:HB, :] = v
            v = g[l, z, y, HB:B].astype(F32)
            for k in range(Y - 1):
                v = v + R2B[m][k].astype(F32)
            gout[m][HB:B, :] = v

    reduces = [{m: Reduce(l, m) for m in names} for l in range(2)]

    def task(l, step, *ms):
        def go():
            for m in ms:
                getattr(reduces[l][m], step)()

        on(l, go)

    def hand_over(l, *ms):
        def go():
            for m in ms:
                reduces[l][m].send()

        on(1 - l, go)

    def column_sum(v):
        return jnp.sum(v, axis=0, keepdims=True)

    def layer_backward(l, dY, at_m, at_c, at_h, at_a):
        DM[l, t] = dY.astype(BF16)
        small[l, 5:6, :] = column_sum(dY)
        wait = gather_x(DM.at[l])
        at_m()
        wait()
        step = F // 2
        for j in range(2):
            cols = slice(j * step, (j + 1) * step)
            dg = nn(rows_of(DM.at[l]), W["p"][l, :, :, :, cols].reshape(D, step))
            DU[:, cols] = (dg * gelu_slope(U[l, :, cols])).astype(BF16)
        total = scatter_x(lambda c: nt(DU[...], weight_rows("f", l, c)))
        grad_matrix("p", l, DM.at[l], lambda: Gl[l])
        hand_over(l, "p")
        grad_matrix("f", l, Cn.at[l], lambda: DU[...])
        hand_over(l, "f")
        small[l, 6:7, :] = column_sum(DU[...].astype(F32))
        at_c()
        dc = total()
        dh = dY + norm_back(dc, N2[l], I2[l], gain(l, 1))
        DH[l, t] = dh.astype(BF16)
        wait = gather_x(DH.at[l])
        small[l, 1:2, :] = column_sum(dc * N2[l])
        small[l, 3:4, :] = column_sum(dc)
        small[l, 4:5, :] = column_sum(dh)
        HID[...] = dh
        at_h()
        wait()
        DO[...] = nn(rows_of(DH.at[l]), weight("o", l)).astype(BF16)
        for pair in range(E // (2 * HD)):
            lo = pair * 2 * HD
            q2 = QKV[l, :, lo : lo + 2 * HD]
            k2 = QKV[l, :, E + lo : E + lo + 2 * HD]
            v2 = QKV[l, :, 2 * E + lo : 2 * E + lo + 2 * HD]
            do2 = DO[:, lo : lo + 2 * HD]
            dq = dk = dv = None
            for h in range(2):
                pr = PR[l, pair * 2 + h]
                p = pr.astype(F32)
                dp = nt(do2, half(v2, h))
                ds = (p * (dp - jnp.sum(p * dp, axis=-1, keepdims=True))).astype(BF16)
                parts = (nn(ds, half(k2, h)), tn(ds, half(q2, h)), tn(pr, half(do2, h)))
                if dq is None:
                    dq, dk, dv = parts
                else:
                    dq, dk, dv = dq + parts[0], dk + parts[1], dv + parts[2]
            DQKV[:, lo : lo + 2 * HD] = (dq * factor).astype(BF16)
            DQKV[:, E + lo : E + lo + 2 * HD] = (dk * factor).astype(BF16)
            DQKV[:, 2 * E + lo : 2 * E + lo + 2 * HD] = dv.astype(BF16)
        total = scatter_x(lambda c: nt(DQKV[...], weight_rows("q", l, c)))
        grad_matrix("q", l, A.at[l], lambda: DQKV[...])
        hand_over(l, "q")
        grad_matrix("o", l, DH.at[l], lambda: O[l])
        hand_over(l, "o")
        small[l, 7:8, :] = jnp.zeros((1, D), F32)
        small[l, 7:8, : 3 * E] = column_sum(DQKV[...].astype(F32))
        at_a()
        da = total()
        small[l, 0:1, :] = column_sum(da * N1[l])
        small[l, 2:3, :] = column_sum(da)
        return HID[...] + norm_back(da, N1[l], I1[l], gain(l, 0))

    class Small:
        def __init__(self, l):
            self.l = l
            mine = small.at[l]
            self.over = copy(mine, small_sib, sibling, 1 - l)
            self.x = [copy(mine, small_x.at[k - 1], at_x(k), l) for k in far_first(T)]
            self.y = [copy(small_x.at[T - 1], small_y.at[k - 1], at_y(k), l) for k in far_first(Y)]
            self.z = [copy(small_y.at[Y - 1], small_z.at[k - 1], at_z(k), l) for k in far_first(Z)]

        def begin(self):
            on(1 - self.l, self.over.start)

        def add(self):
            l = self.l
            self.over.wait_recv()
            small[l] = small[l] + small_sib[...]
            for c in self.x:
                c.start()

        def over_x(self):
            for c in self.x:
                c.wait_recv()
            v = small_x[0]
            for k in range(1, T - 1):
                v = v + small_x[k]
            row = lax.broadcasted_iota(jnp.int32, v.shape, 0)
            small_x[T - 1] = small[self.l] + jnp.where(row < 6, v, 0.0)
            for c in self.y:
                c.start()

        def over_y(self):
            for c in self.y:
                c.wait_recv()
            v = small_x[T - 1]
            for k in range(Y - 1):
                v = v + small_y[k]
            small_y[Y - 1] = v
            for c in self.z:
                c.start()

        def over_z(self):
            for c in self.z:
                c.wait_recv()
            v = small_y[Y - 1]
            for k in range(Z - 1):
                v = v + small_z[k]
            small_out[...] = v

    smalls = [Small(l) for l in range(2)]

    def small_task(l, step):
        on(l, getattr(smalls[l], step))

    act_copy = copy(act_send, act_recv, sibling)
    ig_copy = copy(ig_send, ig_recv, sibling)

    def nothing():
        pass

    def f0_a():
        phase(0, "two", "q", "o")

    def f0_b():
        phase(0, "two", "f", "p")
        phase(1, "one", "q", "o", "f", "p")

    def f0_c():
        phase(1, "two", "q")

    def f0_d():
        phase(1, "two", "o", "f", "p")

    y0 = layer_forward(0, x_in[s].astype(F32), f0_a, f0_b, f0_c, f0_d)
    act0 = y0.astype(BF16)

    @pl.when(s == 0)
    def _():
        act_out[0] = act0

    @pl.when(s == 1)
    def _():
        act_send[...] = act0
        act_copy.start()

    y1 = layer_forward(1, act0.astype(F32), nothing, nothing, nothing, nothing)
    act1 = y1.astype(BF16)

    @pl.when(s == 1)
    def _():
        act_out[1] = act1

    @pl.when(s == 0)
    def _():
        act_send[...] = act1
        act_copy.start()

    def b1_h():
        task(1, "add", "p")

    def b1_a():
        task(1, "add", "f")

    ig1 = layer_backward(1, cot_in[s].astype(F32) * valid, nothing, nothing, b1_h, b1_a).astype(BF16)
    smalls[1].begin()

    @pl.when(s == 1)
    def _():
        grad_out[1] = ig1

    @pl.when(s == 0)
    def _():
        ig_send[...] = ig1
        ig_copy.start()

    def b0_m():
        task(1, "add", "q", "o")
        small_task(1, "add")

    def b0_c():
        task(1, "middle", "p", "f")
        small_task(1, "over_x")

    def b0_h():
        task(1, "middle", "q", "o")
        small_task(1, "over_y")
        task(0, "add", "p")

    def b0_a():
        task(1, "last", *names)
        small_task(1, "over_z")
        task(0, "add", "f")
        task(0, "middle", "p")

    ig0 = layer_backward(0, ig1.astype(F32) * valid, b0_m, b0_c, b0_h, b0_a).astype(BF16)
    smalls[0].begin()

    @pl.when(s == 0)
    def _():
        grad_out[0] = ig0

    @pl.when(s == 1)
    def _():
        ig_send[...] = ig0
        ig_copy.start()

    task(0, "add", "q", "o")
    small_task(0, "add")
    task(0, "middle", "f")
    small_task(0, "over_x")
    task(0, "middle", "q", "o")
    small_task(0, "over_y")
    task(0, "last", *names)
    small_task(0, "over_z")

    act_copy.wait_recv()
    act_out[1 - s] = act_recv[...]
    ig_copy.wait_recv()
    grad_out[1 - s] = ig_recv[...]

    groups = {}
    for c, when in drains:
        groups.setdefault(when, []).append(c)
    for when, copies in groups.items():

        def drain(copies=copies):
            for c in copies:
                c.wait_send()

        if when is None:
            drain()
        else:
            on(when, drain)
    assert count[0] <= n_sems, count[0]


def split_dp(n):
    root = int(round(n**0.5))
    return n // root, root


def fused(sz, x, cot, shards, pack, seqs):
    names = sz.names
    Z, Y, T, LR, D, E, F, R = sz.Z, sz.Y, sz.T, sz.LR, sz.D, sz.E, sz.F, sz.R
    wd = sz.width
    n_sems = 400
    vm = pltpu.VMEM
    scratch = (
        [vm((2, Z, Y, sz.B, wd[m]), BF16) for m in names]
        + [vm((2, Z, Y, sz.B, wd[m]), BF16) for m in names]
        + [vm((Z, Y, sz.B, wd[m]), BF16) for m in names]
        + [vm((Y - 1, Z, sz.HB, wd[m]), BF16) for m in names]
        + [vm((Z - 1, Y, sz.HB, wd[m]), BF16) for m in names]
        + [vm((Z - 1, sz.HB, wd[m]), BF16) for m in names]
        + [vm((Y - 1, sz.HB, wd[m]), BF16) for m in names]
        + [vm((2, 8, D), F32)]
        + [vm((2, T, LR, D), BF16)] * 4
        + [
            vm((2, R, 3 * E), BF16),
            vm((2, R, E), BF16),
            vm((2, E // HD, R, R), BF16),
            vm((2, R, F), F32),
            vm((2, R, F), BF16),
        ]
        + [vm((R, F), BF16), vm((R, E), BF16), vm((R, 3 * E), BF16)]
        + [vm((2, LR, D), F32), vm((2, LR, 1), F32), vm((2, LR, D), F32), vm((2, LR, 1), F32)]
        + [vm((LR, D), F32), vm((R, R), F32)]
        + [vm((2, sz.C, T, LR, sz.DC), BF16), vm((8, sz.C, T - 1, LR, sz.DC), BF16)]
        + [
            vm((2, 8, D), F32),
            vm((8, D), F32),
            vm((T, 8, D), F32),
            vm((Y, 8, D), F32),
            vm((Z, 8, D), F32),
        ]
        + [vm((LR, D), BF16)] * 4
        + [pltpu.SemaphoreType.DMA((n_sems,)), pltpu.SemaphoreType.DMA((n_sems,))]
    )
    sds = jax.ShapeDtypeStruct
    out_shape = (
        [sds((2, LR, D), BF16), sds((2, LR, D), BF16)]
        + [sds((sz.B, wd[m]), F32) for m in names]
        + [sds((8, D), F32)]
    )
    spec = pl.BlockSpec(memory_space=pltpu.VMEM)

    def body(*refs):
        kernel_body(sz, n_sems, *refs)

    return pl.pallas_call(
        body,
        out_shape=out_shape,
        in_specs=[spec] * 8,
        out_specs=[spec] * 7,
        scratch_shapes=scratch,
        compiler_params=pltpu.CompilerParams(
            collective_id=0, has_side_effects=True, vmem_limit_bytes=62 << 20
        ),
        name="layers",
    )(x, cot, *shards, pack, seqs)


def per_device(
    inputs,
    cotangent,
    w_qkv,
    b_qkv,
    w_out,
    w_fc,
    b_fc,
    w_proj,
    norm_gains,
    norm_shifts,
    seq_lengths,
    seq_ranks,
    seq_micros,
):
    Z, Y = split_dp(lax.axis_size("dp"))
    T = lax.axis_size("tensor")
    E = w_qkv.shape[3]
    D = inputs.shape[2]
    sz = Sizes(Z, Y, T, inputs.shape[1], D, E, w_fc.shape[2])
    shards = [w_qkv[0].reshape(-1, 3 * E), w_out[0].T, w_fc[0], w_proj[0].T]
    pack = jnp.concatenate(
        [
            norm_gains[0],
            norm_shifts[0],
            jnp.pad(b_fc, ((0, 0), (0, D - b_fc.shape[1]))),
            jnp.pad(b_qkv.reshape(1, 3 * E), ((0, 0), (0, D - 3 * E))),
        ],
        axis=0,
    )
    seqs = jnp.stack([seq_lengths, seq_ranks, seq_micros])
    act, grad, gq, go, gf, gp, small = fused(sz, inputs, cotangent, shards, pack, seqs)
    return (
        act[None],
        grad[None],
        gq.reshape(1, -1, 3, E),
        small[7:8, : 3 * E].reshape(1, 3, E),
        go.T[None],
        gf[None],
        small[6:7, : b_fc.shape[1]],
        gp.T[None],
        small[None, :2],
        small[None, 2:6],
    )


def solution(mesh):
    placed = (
        P(None, ("dp", "tensor"), None),
        P(None, ("dp", "tensor"), None),
        P("section", "dp", None, "tensor"),
        P("section", None, "tensor"),
        P("section", "tensor", "dp"),
        P("section", "dp", "tensor"),
        P("section", "tensor"),
        P("section", "tensor", "dp"),
        P("section", None, None),
        P("section", None, None),
        P(),
        P(),
        P(),
    )
    return jax.shard_map(
        per_device,
        mesh=mesh,
        in_specs=placed,
        out_specs=(
            P("section", None, ("dp", "tensor"), None),
            P("section", None, ("dp", "tensor"), None),
            P("section", "dp", None, "tensor"),
            P("section", None, "tensor"),
            P("section", "tensor", "dp"),
            P("section", "dp", "tensor"),
            P("section", "tensor"),
            P("section", "tensor", "dp"),
            P("section", None, None),
            P("section", None, None),
        ),
        check_vma=False,
    )
```

time: 904 us -> 201 us (0.22); the launches traced: 894 us -> 200 us
  waiting for transfers between devices: 450 us -> 0 us
  blocking collectives: 275 us -> 0 us
  Pallas kernels: 0 us -> 184 us
  matrix products: 65.4 us -> 0 us
  other arithmetic: 60.8 us -> 1.22 us
  between operations: 16.4 us -> 0.7 us
    reduce_scatter x16 -> x0, waiting for transfers between devices: 369 us -> none  [the longest x6 84.2 us: sum_grads(): lax.psum_scatter(values.astype(jnp.bfloat16), 'tensor', scatter_dimension...]
    all_gather x13 -> x0, blocking collectives: 185 us -> none  [the longest x6 79.9 us: gather_grads(): return lax.all_gather(values, 'tensor', axis=0, tiled=True)]
    pallas_call x0 -> x1, Pallas kernels: none -> 184 us  [fused(): pl.pallas_call(body, out_shape=out_shape, in_specs=[spec] * 8, out_specs=...]
    psum x2 -> x0, blocking collectives: 90.1 us -> none  [the longest x1 75.1 us: per_device(): lax.psum((small_sum[0], small_sum[1], norm_total), 'dp')]
    all_gather x3 -> x0, waiting for transfers between devices: 76.7 us -> none  [the longest x1 44.2 us: fetch_weights(): lax.all_gather(w_proj[0], 'dp', axis=1, tiled=True)]
    dot_general x53 -> x0, matrix products: 65.4 us -> none  [the longest x3 8.57 us: layer_forward(): jnp.dot(activated, w_proj_all, preferred_element_type=jnp.float32)]
    reduce_sum x24 -> x0, other arithmetic: 24.4 us -> none  [the longest x6 4.81 us: norm_forward(): jnp.mean(centered * centered, axis=-1, keepdims=True) + epsilon]
    convert_element_type x16 -> x0, other arithmetic: 10.7 us -> none  [the longest x3 3.73 us: layer_backward(): grad_mixed_rows = gather_grads(grad_hidden.astype(jnp.bfloat16))]
  transfers between devices with their start and end apart: 23 -> 0, of which waited for: 19 -> 0; matrix products, arithmetic and copies ran while one was open for 8% -> 0% of each run, Pallas kernels for 0% -> 0%
where the time goes in v1:
time: 201 us; the launch traced here: 200 us
  Pallas kernels  184 us (92%)
  local copies, waits for them, and re-layouts  14.7 us (7%)
    pallas_call x1, Pallas kernels, fused(): pl.pallas_call(body, out_shape=out_shape, in_specs=[spec] * 8, out_specs=...  184 us
    unnamed x32, local copies, waits for them, and re-layouts  8.3 us

profile of v1, /device:TPU:0, one launch (start us, length us, event | category | flops | bytes accessed | tf_op | source)
XLA Modules:
  0.0 200.5 jit_solution(11317387048775195385)
XLA Ops:
  0.6 1.0 copy.26
  1.6 0.7 copy.29
  2.3 0.0 copy-done.5
  2.3 0.6 copy-done.7
  3.0 0.6 select_maximum_fusion.refs_6_
  3.6 0.6 copy-done.9
  4.3 0.0 copy-done.10
  4.3 0.6 pad_add_fusion.refs_7_
  4.9 183.8 %layers.1 = (bf16[2,64,1024]{2,1,0:T(8,128)(2,1)}, bf16[2,64,1024]{2,1,0:T(8,128)(2,1)}, f32[64,768]{1,0:T(8,128)}, f32[64,256]{1,0:T(8,128)}, f32[64,1024]{1,0:...) custom-call(bf16[2,64,1024]{2,1,0:T(8,128)(2,1)} %refs_0_.1, bf16[2,64,1024]{2,1,0:T(8,128)(2,1)} %refs_1_.1, ...), custom_call_target="tpu_custom_call" | custom-call | tf_op jit(solution)/shard_map/layers/pallas_call | solution.py:752
  188.7 1.4 slice_bitcast_fusion
  190.1 1.4 slice_bitcast_fusion.1
  191.5 1.4 slice.13
  192.8 1.3 slice.12
  194.1 1.0 reshape.30
  195.2 0.7 copy.27
  195.9 0.3 copy-done.3
  196.2 0.7 copy.35
  196.9 0.3 copy-done.2
  197.2 0.7 copy.36
  197.9 0.2 copy-done.4
  198.1 0.6 copy.37
  198.7 0.7 copy.38
  199.4 0.3 copy-done
  199.8 0.7 copy.39
  (16 shorter events, 0.1 us)
Async XLA Ops:
  1.6 0.7 copy-start.5
  1.6 0.7 copy-start.6
  2.3 0.7 copy-start.7
  2.3 0.7 copy-start.8
  3.6 0.7 copy-start.9
  3.6 0.7 copy-start.10
  3.6 0.7 copy-start.11
  195.2 1.0 copy-start.3
  196.2 1.0 copy-start.2
  197.2 0.9 copy-start.4
  197.2 1.5 copy-start.1
  198.7 1.0 copy-start

commit v2 on v1

--- a/solution.py
+++ b/solution.py
@@ -61,8 +61,8 @@
         self.DC = width // self.C
         self.B = width // (z * y)
         self.HB = self.B // 2
-        self.names = ("q", "o", "f", "p")
-        self.width = {"q": 3 * heads, "o": heads, "f": hidden, "p": hidden}
+        self.names = ("a", "f", "p")
+        self.width = {"a": 4 * heads, "f": hidden, "p": hidden}
 
 
 def kernel_body(sz, n_sems, *refs):
@@ -70,19 +70,28 @@
     Z, Y, T, LR, D, E, F, R = sz.Z, sz.Y, sz.T, sz.LR, sz.D, sz.E, sz.F, sz.R
     C, DC, HB, B = sz.C, sz.DC, sz.HB, sz.B
     it = iter(refs)
-    x_in, cot_in = next(it), next(it)
-    shard = {m: next(it) for m in names}
-    pack_in, seq_in = next(it), next(it)
-    act_out, grad_out = next(it), next(it)
-    gout = {m: next(it) for m in names}
-    small_out = next(it)
+    x_in, cot_in, wq_in, bq_in, wo_in, wf_in, bf_in, wp_in, gains_in, shifts_in = (
+        next(it) for _ in range(10)
+    )
+    len_in, rank_in, micro_in = next(it), next(it), next(it)
+    act_out, grad_out, gq_out, gbq_out, go_out, gf_out, gbf_out, gp_out, gg_out, gs_out = (
+        next(it) for _ in range(10)
+    )
+
+    def put(m, rows, v):
+        if m == "a":
+            for c in range(3):
+                gq_out[c, rows, :] = v[:, c * E : (c + 1) * E]
+            go_out[rows, :] = v[:, 3 * E :]
+        else:
+            (gf_out if m == "f" else gp_out)[rows, :] = v
+
     W = {m: next(it) for m in names}
     G = {m: next(it) for m in names}
     SIB = {m: next(it) for m in names}
     RA = {m: next(it) for m in names}
-    RB = {m: next(it) for m in names}
-    R2A = {m: next(it) for m in names}
-    R2B = {m: next(it) for m in names}
+    R2 = {m: next(it) for m in names}
+    FIN = {m: next(it) for m in names}
     pack = next(it)
     A, Cn, DM, DH = next(it), next(it), next(it), next(it)
     QKV, O, PR, U, Gl = next(it), next(it), next(it), next(it), next(it)
@@ -101,21 +110,39 @@
     z = d // Y
     y = d % Y
     count = [0]
+    shared = {}
     drains = []
 
-    def copy(src, dst, device, when=None):
-        i = count[0]
-        count[0] += 1
-        c = pltpu.make_async_remote_copy(
-            src_ref=src,
-            dst_ref=dst,
-            send_sem=send_sem.at[i],
-            recv_sem=recv_sem.at[i],
-            device_id=device,
-            device_id_type=MESH,
-        )
-        drains.append((c, when))
-        return c
+    class Move:
+        def __init__(self, src, dst, device, when=None, key=None):
+            i = shared.get(key)
+            if i is None:
+                i = count[0]
+                count[0] += 1
+                if key is not None:
+                    shared[key] = i
+            self.when = when
+            self.made = pltpu.make_async_remote_copy(
+                src_ref=src,
+                dst_ref=dst,
+                send_sem=send_sem.at[i],
+                recv_sem=recv_sem.at[i],
+                device_id=device,
+                device_id_type=MESH,
+            )
+
+        def start(self):
+            self.made.start()
+            if self not in drains:
+                drains.append(self)
+
+        def wait_recv(self):
+            self.made.wait_recv()
+
+        def wait_send(self):
+            self.made.wait_send()
+
+    copy = Move
 
     def at_x(k):
         return (s, d, (t + k) % T)
@@ -141,78 +168,123 @@
     for p in peers:
         pl.semaphore_signal(barrier, inc=1, device_id=p, device_id_type=MESH)
 
-    for m in names:
-        W[m][s, z, y] = shard[m][...]
-    pack[s] = pack_in[...]
+    for c in range(3):
+        W["a"][s, z, y, :, c * E : (c + 1) * E] = wq_in[c]
+        pack[s, 7:8, c * E : (c + 1) * E] = bq_in[:, c * E : (c + 1) * E]
+    W["a"][s, z, y, :, 3 * E :] = wo_in[...]
+    W["f"][s, z, y] = wf_in[...]
+    W["p"][s, z, y] = wp_in[...]
+    pack[s, 0:2, :] = gains_in[...]
+    pack[s, 2:6, :] = shifts_in[...]
+    pack[s, 6:7, :F] = bf_in[...]
     pl.semaphore_wait(barrier, len(peers))
 
     pack_copy = copy(pack.at[s], pack.at[s], sibling)
     pack_copy.start()
+
+    def on(core, f):
+        pl.when(s == core)(f)
 
     class Gather:
         def __init__(self, l, m):
             w = W[m]
-            self.one_a = [
-                copy(w.at[l, z, y, pl.ds(0, HB)], w.at[l, z, y, pl.ds(0, HB)], at_y(k), l)
-                for k in far_first(Y)
-            ]
-            self.one_b = [
-                copy(w.at[l, z, y, pl.ds(HB, HB)], w.at[l, z, y, pl.ds(HB, HB)], at_z(k), l)
-                for k in far_first(Z)
-            ]
-            self.two_a = [
-                copy(w.at[l, z, :, pl.ds(0, HB)], w.at[l, z, :, pl.ds(0, HB)], at_z(k), l)
-                for k in far_first(Z)
-            ]
-            self.two_b = [
-                copy(w.at[l, :, y, pl.ds(HB, HB)], w.at[l, :, y, pl.ds(HB, HB)], at_y(k), l)
-                for k in far_first(Y)
-            ]
-            self.over = copy(w.at[l], w.at[l], sibling, l)
-
-        def one(self):
-            for c in self.one_a + self.one_b:
+            self.l = l
+            half = [pl.ds(0, HB), pl.ds(HB, HB)]
+
+            def same(view, device, when, *key):
+                return copy(view, view, device, when, ("gather", l, m) + key)
+
+            give = w.at[l, z, y, half[1 - l]]
+            self.zero = same(give, sibling, l, 0)
+            zs = [(z + k) % Z for k in range(Z)]
+            ys = [(y + k) % Y for k in range(Y)]
+            self.one, self.two, self.far, self.over = [], [], [], []
+            for h in range(2):
+                own = w.at[l, z, y, half[h]]
+                if h == 0:
+                    n, m_, at_one, at_two, ring = Y, Z, at_y, at_z, zs
+
+                    def strip(i, lo=0, size=Y, ring=ring, h=h):
+                        return w.at[l, ring[i], pl.ds(lo, size), half[h]]
+
+                else:
+                    n, m_, at_one, at_two, ring = Z, Y, at_z, at_y, ys
+
+                    def strip(i, lo=0, size=Z, ring=ring, h=h):
+                        return w.at[l, pl.ds(lo, size), ring[i], half[h]]
+
+                self.one.append([same(own, at_one(k), h, 1, k) for k in far_first(n)])
+                self.two.append({k: same(strip(0), at_two(k), h, 2, k) for k in (1, m_ - 1)})
+                self.far.append(
+                    {
+                        1: same(strip(m_ - 1, 0, n // 2), at_two(1), h, 3, 1),
+                        m_ - 1: same(strip(1, n // 2, n // 2), at_two(m_ - 1), h, 3, 2),
+                    }
+                )
+                if h == l:
+                    first = [same(strip(0), sibling, h, 4, 0)]
+                else:
+                    at = [(z, (y + k) % Y) if h == 0 else ((z + k) % Z, y) for k in range(1, n)]
+                    first = [
+                        same(w.at[l, zz, yy, half[h]], sibling, h, 4, 0, k)
+                        for k, (zz, yy) in enumerate(at)
+                    ]
+                self.over.append([first] + [[same(strip(i), sibling, h, 4, i)] for i in range(1, m_)])
+
+        def s0(self):
+            on(self.l, self.zero.start)
+
+        def s1(self, h):
+            if h != self.l:
+                self.zero.wait_recv()
+            for c in self.one[h]:
                 c.start()
 
-        def two(self):
-            for c in self.one_a:
+        def s2(self, h):
+            for c in self.one[h]:
                 c.wait_recv()
-            for c in self.two_a:
+            for c in self.two[h].values():
                 c.start()
-            for c in self.one_b:
+            for c in self.over[h][0]:
+                c.start()
+
+        def s3(self, h):
+            for k, c in self.two[h].items():
                 c.wait_recv()
-            for c in self.two_b:
-                c.start()
-
-        def three(self):
-            for c in self.two_a + self.two_b:
+                self.far[h][k].start()
+                self.over[h][1 if k != 1 else len(self.over[h]) - 1][0].start()
+
+        def s4(self, h):
+            for c in self.far[h].values():
                 c.wait_recv()
-            self.over.start()
-
-        def arrive(self):
-            self.over.wait_recv()
+            self.over[h][2][0].start()
+
+        def s5(self, h):
+            for group in self.over[1 - h]:
+                for c in group:
+                    c.wait_recv()
 
     gathers = [{m: Gather(l, m) for m in names} for l in range(2)]
 
-    def on(core, f):
-        pl.when(s == core)(f)
-
-    def phase(l, step, *ms):
-        def go():
-            for m in ms:
-                getattr(gathers[l][m], step)()
-
-        on(l, go)
+    def phase(l, *steps):
+        for h in range(2):
+
+            def go(h=h):
+                for one in steps:
+                    getattr(gathers[l][one[0]], one[1:])(h)
+
+            on(h, go)
 
     def ready(l, m):
-        on(l, gathers[l][m].three)
-        on(1 - l, gathers[l][m].arrive)
-
-    phase(0, "one", "q", "o", "f", "p")
-
-    seqs = seq_in[...].astype(F32)
-    n_seq = seqs.shape[1]
-    lengths, ranks, micros = seqs[0:1], seqs[1:2], seqs[2:3]
+        phase(l, m + "s5")
+
+    for l in range(2):
+        for m in names:
+            gathers[l][m].s0()
+    phase(0, "as1", "fs1", "ps1")
+
+    lengths, ranks, micros = (r[...].astype(F32) for r in (len_in, rank_in, micro_in))
+    n_seq = lengths.shape[1]
     mine_row = jnp.logical_and(ranks == d.astype(F32), micros == s.astype(F32))
     taken_row = jnp.where(mine_row, lengths, 0.0)
     i0 = lax.broadcasted_iota(jnp.int32, (n_seq, n_seq), 0)
@@ -247,10 +319,24 @@
     def shift(l, i):
         return pack[l, 2 + i : 3 + i, :]
 
+    turns = [[], []]
+    turn = [0]
+
+    def next_turn():
+        slot = turn[0] % 2
+        turn[0] += 1
+        for c in turns[slot]:
+            c.wait_send()
+            drains.remove(c)
+        turns[slot] = []
+        return slot
+
     def gather_x(buf):
-        copies = [copy(buf.at[t], buf.at[t], at_x(k)) for k in far_first(T)]
+        slot = next_turn()
+        copies = [copy(buf.at[t], buf.at[t], at_x(k), None, ("x", slot, 0, k)) for k in far_first(T)]
         for c in copies:
             c.start()
+        turns[slot] = copies
 
         def wait():
             for c in copies:
@@ -258,33 +344,35 @@
 
         return wait
 
-    stage_busy = {}
-    stage_turn = [0]
+    scatters = [0]
 
     def scatter_x(part):
-        turn = stage_turn[0]
-        stage_turn[0] += 1
-        slot = turn % 2
-        for c in stage_busy.get(slot, []):
-            c.wait_send()
-            drains[:] = [p for p in drains if p[0] is not c]
+        slot = next_turn()
+        number = scatters[0]
+        scatters[0] += 1
         copies = []
         for c in range(C):
-            stage[slot, c] = part(c).astype(BF16).reshape(T, LR, DC)
+            stage[number % 2, c] = part(c).astype(BF16).reshape(T, LR, DC)
             for k in far_first(T):
-                one = copy(stage.at[slot, c, (t + k) % T], recv.at[turn, c, k - 1], at_x(k))
+                one = copy(
+                    stage.at[number % 2, c, (t + k) % T],
+                    recv.at[number, c, k - 1],
+                    at_x(k),
+                    None,
+                    ("x", slot, c, k),
+                )
                 one.start()
                 copies.append(one)
-        stage_busy[slot] = copies
+        turns[slot] = copies
 
         def total():
             for c in copies:
                 c.wait_recv()
             out = []
             for c in range(C):
-                v = stage[slot, c, t].astype(F32)
+                v = stage[number % 2, c, t].astype(F32)
                 for k in range(1, T):
-                    v = v + recv[turn, c, k - 1].astype(F32)
+                    v = v + recv[number, c, k - 1].astype(F32)
                 out.append(v)
             return jnp.concatenate(out, axis=1)
 
@@ -301,24 +389,29 @@
     def rows_of(buf):
         return buf[...].reshape(R, D)
 
+    parts_of = {"q": ("a", 0, 3 * E), "o": ("a", 3 * E, 4 * E), "f": ("f", 0, F), "p": ("p", 0, F)}
+
     def weight(m, l):
-        return W[m][l].reshape(D, sz.width[m])
+        w, lo, hi = parts_of[m]
+        return W[w][l, :, :, :, lo:hi].reshape(D, hi - lo)
 
     def weight_rows(m, l, c):
+        w, lo, hi = parts_of[m]
         span = Z // C
-        return W[m][l, c * span : (c + 1) * span].reshape(DC, sz.width[m])
-
-    def layer_forward(l, X, at_a, at_b, at_c, at_d):
+        return W[w][l, c * span : (c + 1) * span, :, :, lo:hi].reshape(DC, hi - lo)
+
+    def layer_forward(l, X, at_a, at_q, at_b, at_c, at_d):
         n1, inv1 = norm(X)
         N1[l] = n1
         I1[l] = inv1
         A[l, t] = (n1 * gain(l, 0) + shift(l, 0)).astype(BF16)
         wait = gather_x(A.at[l])
         at_a()
-        ready(l, "q")
+        ready(l, "a")
         wait()
         bias = pack[l, 7:8, : 3 * E]
         QKV[l] = (nn(rows_of(A.at[l]), weight("q", l)) + bias).astype(BF16)
+        at_q()
         for pair in range(E // (2 * HD)):
             lo = pair * 2 * HD
             q2 = QKV[l, :, lo : lo + 2 * HD]
@@ -334,7 +427,6 @@
                 part = nn(pr, half(v2, h))
                 o2 = part if o2 is None else o2 + part
             O[l, :, lo : lo + 2 * HD] = o2.astype(BF16)
-        ready(l, "o")
         total = scatter_x(lambda c: nt(O[l], weight_rows("o", l, c)))
         at_b()
         hidden = X + total() + shift(l, 2)
@@ -360,11 +452,12 @@
 
     def grad_matrix(m, l, left, right):
         span = D // Z
+        w, lo, hi = parts_of[m]
 
         def step(i, carry):
             cols = pl.ds(pl.multiple_of(i * span, span), span)
             block = tn(left[:, :, cols].reshape(R, span), right())
-            G[m][l, i] = block.astype(BF16).reshape(Y, B, sz.width[m])
+            G[w][l, i, :, :, lo:hi] = block.astype(BF16).reshape(Y, B, hi - lo)
             return carry
 
         lax.fori_loop(0, Z, step, 0)
@@ -373,88 +466,95 @@
         def __init__(self, l, m):
             self.l, self.m = l, m
             g = G[m]
-            self.over = copy(g.at[l], SIB[m], sibling, 1 - l)
-            self.one_a = [
-                copy(g.at[l, :, (y + k) % Y, pl.ds(0, HB)], RA[m].at[k - 1], at_y(k), l)
-                for k in far_first(Y)
+            half = [pl.ds(0, HB), pl.ds(HB, HB)]
+            self.over = [
+                copy(g.at[l, :, :, half[1 - h]], SIB[m].at[l], sibling, h, (l, m, 0)) for h in range(2)
             ]
-            self.one_b = [
-                copy(g.at[l, (z + k) % Z, :, pl.ds(HB, HB)], RB[m].at[k - 1], at_z(k), l)
-                for k in far_first(Z)
+            self.one = [
+                [
+                    copy(g.at[l, :, (y + k) % Y, half[0]], RA[m].at[l, k - 1], at_y(k), 0, (l, m, 1, k))
+                    for k in far_first(Y)
+                ],
+                [
+                    copy(g.at[l, (z + k) % Z, :, half[1]], RA[m].at[l, k - 1], at_z(k), 1, (l, m, 1, k))
+                    for k in far_first(Z)
+                ],
             ]
-            self.two_a = [
-                copy(g.at[l, (z + k) % Z, y, pl.ds(0, HB)], R2A[m].at[k - 1], at_z(k), l)
-                for k in far_first(Z)
+            self.two = [
+                [
+                    copy(g.at[l, (z + k) % Z, y, half[0]], R2[m].at[l, k - 1], at_z(k), 0, (l, m, 2, k))
+                    for k in far_first(Z)
+                ],
+                [
+                    copy(g.at[l, z, (y + k) % Y, half[1]], R2[m].at[l, k - 1], at_y(k), 1, (l, m, 2, k))
+                    for k in far_first(Y)
+                ],
             ]
-            self.two_b = [
-                copy(g.at[l, z, (y + k) % Y, pl.ds(HB, HB)], R2B[m].at[k - 1], at_y(k), l)
-                for k in far_first(Y)
-            ]
-
-        def send(self):
-            self.over.start()
-
-        def add(self):
+            self.back = copy(FIN[m].at[0], FIN[m].at[1], sibling, 1 - l)
+
+        def r0(self, h):
+            self.over[h].start()
+
+        def r1(self, h):
             g, l, m = G[self.m], self.l, self.m
-            self.over.wait_recv()
+            rows = slice(h * HB, h * HB + HB)
+            self.over[1 - h].wait_recv()
 
             def step(i, carry):
-                g[l, i] = (g[l, i].astype(F32) + SIB[m][i].astype(F32)).astype(BF16)
+                g[l, i, :, rows] = (g[l, i, :, rows].astype(F32) + SIB[m][l, i].astype(F32)).astype(BF16)
                 return carry
 
             lax.fori_loop(0, Z, step, 0)
-            for c in self.one_a + self.one_b:
+            for c in self.one[h]:
                 c.start()
 
-        def middle(self):
+        def r2(self, h):
             g, l, m = G[self.m], self.l, self.m
-            for c in self.one_a:
+            rows = slice(h * HB, h * HB + HB)
+            for c in self.one[h]:
                 c.wait_recv()
-            for i in range(Z):
-                v = g[l, i, y, 0:HB].astype(F32)
-                for k in range(Y - 1):
-                    v = v + RA[m][k, i].astype(F32)
-                g[l, i, y, 0:HB] = v.astype(BF16)
-            for c in self.two_a:
+            n = len(self.one[h])
+            for i in range(n + 1):
+                at = (l, i, y, rows) if h == 0 else (l, z, i, rows)
+                v = g[at].astype(F32)
+                for k in range(n):
+                    v = v + RA[m][l, k, i].astype(F32)
+                g[at] = v.astype(BF16)
+            for c in self.two[h]:
                 c.start()
-            for c in self.one_b:
+
+        def r3(self, h):
+            g, l, m = G[self.m], self.l, self.m
+            rows = slice(h * HB, h * HB + HB)
+            for c in self.two[h]:
                 c.wait_recv()
-            for i in range(Y):
-                v = g[l, z, i, HB:B].astype(F32)
-                for k in range(Z - 1):
-                    v = v + RB[m][k, i].astype(F32)
-                g[l, z, i, HB:B] = v.astype(BF16)
-            for c in self.two_b:
-                c.start()
-
-        def last(self):
-            g, l, m = G[self.m], self.l, self.m
-            for c in self.two_a + self.two_b:
-                c.wait_recv()
-            v = g[l, z, y, 0:HB].astype(F32)
-            for k in range(Z - 1):
-                v = v + R2A[m][k].astype(F32)
-            gout[m][0:HB, :] = v
-            v = g[l, z, y, HB:B].astype(F32)
-            for k in range(Y - 1):
-                v = v + R2B[m][k].astype(F32)
-            gout[m][HB:B, :] = v
+            v = g[l, z, y, rows].astype(F32)
+            for k in range(len(self.two[h])):
+                v = v + R2[m][l, k].astype(F32)
+            if h == l:
+                put(m, rows, v)
+            else:
+                FIN[m][0] = v
+                self.back.start()
+
+        def r4(self, h):
+            if h == self.l:
+                self.back.wait_recv()
+                put(self.m, slice((1 - h) * HB, (2 - h) * HB), FIN[self.m][1])
 
     reduces = [{m: Reduce(l, m) for m in names} for l in range(2)]
 
-    def task(l, step, *ms):
-        def go():
-            for m in ms:
-                getattr(reduces[l][m], step)()
-
-        on(l, go)
-
-    def hand_over(l, *ms):
-        def go():
-            for m in ms:
-                reduces[l][m].send()
-
-        on(1 - l, go)
+    def task(l, *steps):
+        for h in range(2):
+
+            def go(h=h):
+                for one in steps:
+                    getattr(reduces[l][one[0]], one[1:])(h)
+
+            on(h, go)
+
+    def hand_over(l, m):
+        task(l, m + "r0")
 
     def column_sum(v):
         return jnp.sum(v, axis=0, keepdims=True)
@@ -510,9 +610,8 @@
             DQKV[:, 2 * E + lo : 2 * E + lo + 2 * HD] = dv.astype(BF16)
         total = scatter_x(lambda c: nt(DQKV[...], weight_rows("q", l, c)))
         grad_matrix("q", l, A.at[l], lambda: DQKV[...])
-        hand_over(l, "q")
         grad_matrix("o", l, DH.at[l], lambda: O[l])
-        hand_over(l, "o")
+        hand_over(l, "a")
         small[l, 7:8, :] = jnp.zeros((1, D), F32)
         small[l, 7:8, : 3 * E] = column_sum(DQKV[...].astype(F32))
         at_a()
@@ -525,10 +624,10 @@
         def __init__(self, l):
             self.l = l
             mine = small.at[l]
-            self.over = copy(mine, small_sib, sibling, 1 - l)
-            self.x = [copy(mine, small_x.at[k - 1], at_x(k), l) for k in far_first(T)]
-            self.y = [copy(small_x.at[T - 1], small_y.at[k - 1], at_y(k), l) for k in far_first(Y)]
-            self.z = [copy(small_y.at[Y - 1], small_z.at[k - 1], at_z(k), l) for k in far_first(Z)]
+            self.over = copy(mine, small_sib, sibling, 1 - l, "small")
+            self.x = [copy(mine, small_x.at[k - 1], at_x(k), l, ("small", 0, k)) for k in far_first(T)]
+            self.y = [copy(small_x.at[T - 1], small_y.at[k - 1], at_y(k), l, ("small", 1, k)) for k in far_first(Y)]
+            self.z = [copy(small_y.at[Y - 1], small_z.at[k - 1], at_z(k), l, ("small", 2, k)) for k in far_first(Z)]
 
         def begin(self):
             on(1 - self.l, self.over.start)
@@ -567,7 +666,10 @@
             v = small_y[Y - 1]
             for k in range(Z - 1):
                 v = v + small_z[k]
-            small_out[...] = v
+            gg_out[...] = v[0:2]
+            gs_out[...] = v[2:6]
+            gbf_out[...] = v[6:7, :F]
+            gbq_out[...] = v[7:8, : 3 * E]
 
     smalls = [Small(l) for l in range(2)]
 
@@ -577,23 +679,33 @@
     act_copy = copy(act_send, act_recv, sibling)
     ig_copy = copy(ig_send, ig_recv, sibling)
 
+    def f0_a():
+        phase(0, "as2", "fs2", "as3", "ps2", "as4")
+
+    def f0_q():
+        phase(0, "fs3")
+
+    def f0_b():
+        phase(0, "ps3", "fs4")
+        phase(1, "as1", "fs1", "ps1")
+
+    def f0_c():
+        phase(0, "ps4")
+        phase(1, "as2", "fs2", "ps2")
+
+    def f0_d():
+        phase(1, "as3", "fs3")
+
+    def f1_a():
+        phase(1, "ps3", "as4")
+
+    def f1_b():
+        phase(1, "fs4", "ps4")
+
     def nothing():
         pass
 
-    def f0_a():
-        phase(0, "two", "q", "o")
-
-    def f0_b():
-        phase(0, "two", "f", "p")
-        phase(1, "one", "q", "o", "f", "p")
-
-    def f0_c():
-        phase(1, "two", "q")
-
-    def f0_d():
-        phase(1, "two", "o", "f", "p")
-
-    y0 = layer_forward(0, x_in[s].astype(F32), f0_a, f0_b, f0_c, f0_d)
+    y0 = layer_forward(0, x_in[s].astype(F32), f0_a, f0_q, f0_b, f0_c, f0_d)
     act0 = y0.astype(BF16)
 
     @pl.when(s == 0)
@@ -605,7 +717,7 @@
         act_send[...] = act0
         act_copy.start()
 
-    y1 = layer_forward(1, act0.astype(F32), nothing, nothing, nothing, nothing)
+    y1 = layer_forward(1, act0.astype(F32), f1_a, nothing, f1_b, nothing, nothing)
     act1 = y1.astype(BF16)
 
     @pl.when(s == 1)
@@ -618,10 +730,10 @@
         act_copy.start()
 
     def b1_h():
-        task(1, "add", "p")
+        task(1, "pr1")
 
     def b1_a():
-        task(1, "add", "f")
+        task(1, "fr1", "pr2")
 
     ig1 = layer_backward(1, cot_in[s].astype(F32) * valid, nothing, nothing, b1_h, b1_a).astype(BF16)
     smalls[1].begin()
@@ -636,23 +748,22 @@
         ig_copy.start()
 
     def b0_m():
-        task(1, "add", "q", "o")
+        task(1, "ar1", "fr2")
         small_task(1, "add")
 
     def b0_c():
-        task(1, "middle", "p", "f")
+        task(1, "ar2", "pr3")
         small_task(1, "over_x")
 
     def b0_h():
-        task(1, "middle", "q", "o")
+        task(1, "fr3")
         small_task(1, "over_y")
-        task(0, "add", "p")
+        task(0, "pr1")
 
     def b0_a():
-        task(1, "last", *names)
+        task(0, "fr1", "pr2")
+        task(1, "ar3")
         small_task(1, "over_z")
-        task(0, "add", "f")
-        task(0, "middle", "p")
 
     ig0 = layer_backward(0, ig1.astype(F32) * valid, b0_m, b0_c, b0_h, b0_a).astype(BF16)
     smalls[0].begin()
@@ -666,14 +777,15 @@
         ig_send[...] = ig0
         ig_copy.start()
 
-    task(0, "add", "q", "o")
+    task(0, "ar1", "fr2")
     small_task(0, "add")
-    task(0, "middle", "f")
     small_task(0, "over_x")
-    task(0, "middle", "q", "o")
+    task(0, "pr3", "ar2")
     small_task(0, "over_y")
-    task(0, "last", *names)
+    task(0, "fr3", "ar3")
     small_task(0, "over_z")
+    for l in range(2):
+        task(l, *(m + "r4" for m in names))
 
     act_copy.wait_recv()
     act_out[1 - s] = act_recv[...]
@@ -681,8 +793,8 @@
     grad_out[1 - s] = ig_recv[...]
 
     groups = {}
-    for c, when in drains:
-        groups.setdefault(when, []).append(c)
+    for c in drains:
+        groups.setdefault(c.when, []).append(c)
     for when, copies in groups.items():
 
         def drain(copies=copies):
@@ -701,20 +813,19 @@
     return n // root, root
 
 
-def fused(sz, x, cot, shards, pack, seqs):
+def fused(sz, arrays, out_shape):
     names = sz.names
     Z, Y, T, LR, D, E, F, R = sz.Z, sz.Y, sz.T, sz.LR, sz.D, sz.E, sz.F, sz.R
     wd = sz.width
-    n_sems = 400
+    n_sems = 168
     vm = pltpu.VMEM
     scratch = (
         [vm((2, Z, Y, sz.B, wd[m]), BF16) for m in names]
         + [vm((2, Z, Y, sz.B, wd[m]), BF16) for m in names]
-        + [vm((Z, Y, sz.B, wd[m]), BF16) for m in names]
-        + [vm((Y - 1, Z, sz.HB, wd[m]), BF16) for m in names]
-        + [vm((Z - 1, Y, sz.HB, wd[m]), BF16) for m in names]
-        + [vm((Z - 1, sz.HB, wd[m]), BF16) for m in names]
-        + [vm((Y - 1, sz.HB, wd[m]), BF16) for m in names]
+        + [vm((2, Z, Y, sz.HB, wd[m]), BF16) for m in names]
+        + [vm((2, Y - 1, Z, sz.HB, wd[m]), BF16) for m in names]
+        + [vm((2, Z - 1, sz.HB, wd[m]), BF16) for m in names]
+        + [vm((2, sz.HB, wd[m]), F32) for m in names]
         + [vm((2, 8, D), F32)]
         + [vm((2, T, LR, D), BF16)] * 4
         + [
@@ -738,12 +849,6 @@
         + [vm((LR, D), BF16)] * 4
         + [pltpu.SemaphoreType.DMA((n_sems,)), pltpu.SemaphoreType.DMA((n_sems,))]
     )
-    sds = jax.ShapeDtypeStruct
-    out_shape = (
-        [sds((2, LR, D), BF16), sds((2, LR, D), BF16)]
-        + [sds((sz.B, wd[m]), F32) for m in names]
-        + [sds((8, D), F32)]
-    )
     spec = pl.BlockSpec(memory_space=pltpu.VMEM)
 
     def body(*refs):
@@ -752,59 +857,71 @@
     return pl.pallas_call(
         body,
         out_shape=out_shape,
-        in_specs=[spec] * 8,
-        out_specs=[spec] * 7,
+        in_specs=[spec] * len(arrays),
+        out_specs=[spec] * len(out_shape),
         scratch_shapes=scratch,
         compiler_params=pltpu.CompilerParams(
             collective_id=0, has_side_effects=True, vmem_limit_bytes=62 << 20
         ),
         name="layers",
-    )(x, cot, *shards, pack, seqs)
-
-
-def per_device(
-    inputs,
-    cotangent,
-    w_qkv,
-    b_qkv,
-    w_out,
-    w_fc,
-    b_fc,
-    w_proj,
-    norm_gains,
-    norm_shifts,
-    seq_lengths,
-    seq_ranks,
-    seq_micros,
-):
+    )(*arrays)
+
+
+def hand_out(arrays):
+    n = len(arrays)
+
+    def body(*refs):
+        sems = refs[2 * n]
+        copies = [pltpu.make_async_copy(refs[i], refs[n + i], sems.at[i]) for i in range(n)]
+        for c in copies:
+            c.start()
+        for c in copies:
+            c.wait()
+
+    return pl.pallas_call(
+        body,
+        out_shape=[jax.ShapeDtypeStruct(a.shape, a.dtype) for a in arrays],
+        in_specs=[pl.BlockSpec(memory_space=pltpu.VMEM)] * n,
+        out_specs=[pl.BlockSpec(memory_space=pl.ANY)] * n,
+        scratch_shapes=[pltpu.SemaphoreType.DMA((n,))],
+        name="hand_out",
+    )(*arrays)
+
+
+def per_device(*arrays):
+    inputs, cotangent, w_qkv, b_qkv, w_out, w_fc, b_fc, w_proj, gains, shifts = arrays[:10]
     Z, Y = split_dp(lax.axis_size("dp"))
     T = lax.axis_size("tensor")
     E = w_qkv.shape[3]
-    D = inputs.shape[2]
-    sz = Sizes(Z, Y, T, inputs.shape[1], D, E, w_fc.shape[2])
-    shards = [w_qkv[0].reshape(-1, 3 * E), w_out[0].T, w_fc[0], w_proj[0].T]
-    pack = jnp.concatenate(
-        [
-            norm_gains[0],
-            norm_shifts[0],
-            jnp.pad(b_fc, ((0, 0), (0, D - b_fc.shape[1]))),
-            jnp.pad(b_qkv.reshape(1, 3 * E), ((0, 0), (0, D - 3 * E))),
-        ],
-        axis=0,
+    sz = Sizes(Z, Y, T, inputs.shape[1], inputs.shape[2], E, w_fc.shape[2])
+    params = [
+        w_qkv[0].transpose(1, 0, 2),
+        b_qkv.reshape(1, 3 * E),
+        w_out[0].T,
+        w_fc[0],
+        b_fc,
+        w_proj[0].T,
+        gains[0],
+        shifts[0],
+    ]
+    seqs = [a.reshape(1, -1) for a in arrays[10:]]
+    out_shape = [jax.ShapeDtypeStruct(inputs.shape, BF16)] * 2 + [
+        jax.ShapeDtypeStruct(a.shape, F32) for a in params
+    ]
+    act, grad, gq, gbq, go, gf, gbf, gp, gg, gs = hand_out(
+        fused(sz, [inputs, cotangent] + params + seqs, out_shape)
     )
-    seqs = jnp.stack([seq_lengths, seq_ranks, seq_micros])
-    act, grad, gq, go, gf, gp, small = fused(sz, inputs, cotangent, shards, pack, seqs)
     return (
         act[None],
         grad[None],
-        gq.reshape(1, -1, 3, E),
-        small[7:8, : 3 * E].reshape(1, 3, E),
+        gq.transpose(1, 0, 2)[None],
+        gbq.reshape(1, 3, E),
         go.T[None],
         gf[None],
-        small[6:7, : b_fc.shape[1]],
+        gbf,
         gp.T[None],
-        small[None, :2],
-        small[None, 2:6],
+        gg[None],
+        gs[None],
     )
 
 

time: 201 us -> 182 us (0.905)
  local copies, waits for them, and re-layouts: 14.7 us -> 0 us
  Pallas kernels: 184 us -> 181 us
    unnamed x32 -> x0, local copies, waits for them, and re-layouts: 8.3 us -> none
    pallas_call x1 -> x2, Pallas kernels: 184 us -> 181 us  [the longest x1 178 us: fused(): pl.pallas_call(body, out_shape=out_shape, in_specs=[spec] * len(arrays),...]
    broadcast_in_dim x2 -> x0, local copies, waits for them, and re-layouts: 2.73 us -> none  [the longest x1 1.37 us: per_device(): small[None, 2:6]]
    slice x2 -> x0, local copies, waits for them, and re-layouts: 2.67 us -> none  [the longest x1 1.35 us: per_device(): small[6:7, :b_fc.shape[1]]]
where the time goes in v2:
time: 182 us
  Pallas kernels  181 us (99%)
    pallas_call x1, Pallas kernels, fused(): pl.pallas_call(body, out_shape=out_shape, in_specs=[spec] * len(arrays),...  178 us

profile of v2, /device:TPU:0, one launch (start us, length us, event | category | flops | bytes accessed | tf_op | source)
XLA Modules:
  0.0 181.6 jit_solution(12698899301638726335)
XLA Ops:
  0.6 178.3 %layers.1 = (bf16[2,64,1024]{2,1,0:T(8,128)(2,1)}, bf16[2,64,1024]{2,1,0:T(8,128)(2,1)}, f32[3,64,256]{2,1,0:T(8,128)}, f32[1,768]{1,0:T(1,128)}, f32[64,256]{1,...) custom-call(bf16[2,64,1024]{2,1,0:T(8,128)(2,1)} %refs_0_.1, ...), custom_call_target="tpu_custom_call" | custom-call | tf_op jit(solution)/shard_map/layers/pallas_call | solution.py:857
  179.0 2.4 %hand_out.1 = (bf16[2,64,1024]{2,1,0:T(8,128)(2,1)}, bf16[2,64,1024]{2,1,0:T(8,128)(2,1)}, f32[3,64,256]{2,1,0:T(8,128)}, f32[1,768]{1,0:T(1,128)}, f32[64,256]{...) custom-call(bf16[2,64,1024]{2,1,0:T(8,128)(2,1)} %get-tuple-element., ...), custom_call_target="tpu_custom_call" | custom-call | tf_op jit(solution)/shard_map/hand_out/pallas_call | solution.py:881

commit v3 on v2

--- a/solution.py
+++ b/solution.py
@@ -57,8 +57,7 @@
         self.Z, self.Y, self.T = z, y, t
         self.LR, self.D, self.E, self.F = rows, width, heads, hidden
         self.R = rows * t
-        self.C = 2
-        self.DC = width // self.C
+        self.HR = rows // 2
         self.B = width // (z * y)
         self.HB = self.B // 2
         self.names = ("a", "f", "p")
@@ -68,7 +67,7 @@
 def kernel_body(sz, n_sems, *refs):
     names = sz.names
     Z, Y, T, LR, D, E, F, R = sz.Z, sz.Y, sz.T, sz.LR, sz.D, sz.E, sz.F, sz.R
-    C, DC, HB, B = sz.C, sz.DC, sz.HB, sz.B
+    HR, HB, B = sz.HR, sz.HB, sz.B
     it = iter(refs)
     x_in, cot_in, wq_in, bq_in, wo_in, wf_in, bf_in, wp_in, gains_in, shifts_in = (
         next(it) for _ in range(10)
@@ -97,7 +96,7 @@
     QKV, O, PR, U, Gl = next(it), next(it), next(it), next(it), next(it)
     DU, DO, DQKV = next(it), next(it), next(it)
     N1, I1, N2, I2 = next(it), next(it), next(it), next(it)
-    HID = next(it)
+    HID, DYS = next(it), next(it)
     MASK = next(it)
     stage, recv = next(it), next(it)
     small, small_sib, small_x, small_y, small_z = next(it), next(it), next(it), next(it), next(it)
@@ -309,7 +308,7 @@
     same = jnp.logical_and(label_col == label_row, label_col > 0.5)
     visible = jnp.logical_or(jnp.logical_and(same, r1 <= r0), r0 == r1)
     MASK[...] = jnp.where(visible, 1.0, 0.0)
-    valid = jnp.where(column_labels(LR, t * LR) > 0.5, 1.0, 0.0)
+    valid = [jnp.where(column_labels(HR, t * LR + h * HR) > 0.5, 1.0, 0.0) for h in range(2)]
 
     pack_copy.wait_recv()
 
@@ -319,24 +318,25 @@
     def shift(l, i):
         return pack[l, 2 + i : 3 + i, :]
 
-    turns = [[], []]
-    turn = [0]
-
-    def next_turn():
-        slot = turn[0] % 2
-        turn[0] += 1
-        for c in turns[slot]:
+    halves = [slice(h * HR, h * HR + HR) for h in range(2)]
+    turns = {(h, slot): [] for h in range(2) for slot in range(3)}
+    turn = [0, 0]
+
+    def next_turn(h):
+        slot = turn[h] % 3
+        turn[h] += 1
+        for c in turns[h, slot]:
             c.wait_send()
             drains.remove(c)
-        turns[slot] = []
         return slot
 
-    def gather_x(buf):
-        slot = next_turn()
-        copies = [copy(buf.at[t], buf.at[t], at_x(k), None, ("x", slot, 0, k)) for k in far_first(T)]
+    def gather_x(buf, h):
+        slot = next_turn(h)
+        part = buf.at[t, pl.ds(h * HR, HR)]
+        copies = [copy(part, part, at_x(k), None, ("x", slot, h, k)) for k in far_first(T)]
         for c in copies:
             c.start()
-        turns[slot] = copies
+        turns[h, slot] = copies
 
         def wait():
             for c in copies:
@@ -344,37 +344,35 @@
 
         return wait
 
-    scatters = [0]
-
-    def scatter_x(part):
-        slot = next_turn()
-        number = scatters[0]
-        scatters[0] += 1
-        copies = []
-        for c in range(C):
-            stage[number % 2, c] = part(c).astype(BF16).reshape(T, LR, DC)
-            for k in far_first(T):
-                one = copy(
-                    stage.at[number % 2, c, (t + k) % T],
-                    recv.at[number, c, k - 1],
-                    at_x(k),
-                    None,
-                    ("x", slot, c, k),
-                )
-                one.start()
-                copies.append(one)
-        turns[slot] = copies
+    scatters = [0, 0]
+
+    def scatter_x(part, h):
+        slot = next_turn(h)
+        number = scatters[h]
+        scatters[h] += 1
+        turned = number % 2
+        stage[turned, h] = part.astype(BF16).reshape(T, HR, D)
+        copies = [
+            copy(
+                stage.at[turned, h, (t + k) % T],
+                recv.at[number, h, k - 1],
+                at_x(k),
+                None,
+                ("x", slot, h, k),
+            )
+            for k in far_first(T)
+        ]
+        for c in copies:
+            c.start()
+        turns[h, slot] = copies
 
         def total():
             for c in copies:
                 c.wait_recv()
-            out = []
-            for c in range(C):
-                v = stage[number % 2, c, t].astype(F32)
-                for k in range(1, T):
-                    v = v + recv[number, c, k - 1].astype(F32)
-                out.append(v)
-            return jnp.concatenate(out, axis=1)
+            v = stage[turned, h, t].astype(F32)
+            for k in range(1, T):
+                v = v + recv[number, h, k - 1].astype(F32)
+            return v
 
         return total
 
@@ -386,8 +384,16 @@
 
     factor = HD ** (-0.5)
 
-    def rows_of(buf):
-        return buf[...].reshape(R, D)
+    def some(buf, l, h, lo=None, hi=None):
+        v = buf[l, :, halves[h], lo:hi]
+        return v.reshape(T * HR, v.shape[-1])
+
+    def every(buf, l, lo=None, hi=None):
+        v = buf[l, :, :, lo:hi]
+        return v.reshape(R, v.shape[-1])
+
+    def spread(v, n):
+        return v.reshape(T, n, v.shape[-1])
 
     parts_of = {"q": ("a", 0, 3 * E), "o": ("a", 3 * E, 4 * E), "f": ("f", 0, F), "p": ("p", 0, F)}
 
@@ -395,28 +401,27 @@
         w, lo, hi = parts_of[m]
         return W[w][l, :, :, :, lo:hi].reshape(D, hi - lo)
 
-    def weight_rows(m, l, c):
-        w, lo, hi = parts_of[m]
-        span = Z // C
-        return W[w][l, c * span : (c + 1) * span, :, :, lo:hi].reshape(DC, hi - lo)
-
-    def layer_forward(l, X, at_a, at_q, at_b, at_c, at_d):
-        n1, inv1 = norm(X)
-        N1[l] = n1
-        I1[l] = inv1
-        A[l, t] = (n1 * gain(l, 0) + shift(l, 0)).astype(BF16)
-        wait = gather_x(A.at[l])
+    def layer_forward(l, inputs_of, at_a, at_q, at_b, at_c, at_d):
+        waits = []
+        for h in range(2):
+            rows = halves[h]
+            X = inputs_of[h]()
+            n1, inv1 = norm(X)
+            N1[l, rows] = n1
+            I1[l, rows] = inv1
+            HID[rows] = X
+            A[l, t, rows] = (n1 * gain(l, 0) + shift(l, 0)).astype(BF16)
+            waits.append(gather_x(A.at[l], h))
         at_a()
         ready(l, "a")
-        wait()
-        bias = pack[l, 7:8, : 3 * E]
-        QKV[l] = (nn(rows_of(A.at[l]), weight("q", l)) + bias).astype(BF16)
+        for h in range(2):
+            waits[h]()
+            v = nn(some(A, l, h), weight("q", l)) + pack[l, 7:8, : 3 * E]
+            QKV[l, :, halves[h], :] = spread(v.astype(BF16), HR)
         at_q()
         for pair in range(E // (2 * HD)):
             lo = pair * 2 * HD
-            q2 = QKV[l, :, lo : lo + 2 * HD]
-            k2 = QKV[l, :, E + lo : E + lo + 2 * HD]
-            v2 = QKV[l, :, 2 * E + lo : 2 * E + lo + 2 * HD]
+            q2, k2, v2 = (every(QKV, l, i * E + lo, i * E + lo + 2 * HD) for i in range(3))
             o2 = None
             for h in range(2):
                 S = nt(q2, half(k2, h)) * factor
@@ -426,29 +431,37 @@
                 PR[l, pair * 2 + h] = pr
                 part = nn(pr, half(v2, h))
                 o2 = part if o2 is None else o2 + part
-            O[l, :, lo : lo + 2 * HD] = o2.astype(BF16)
-        total = scatter_x(lambda c: nt(O[l], weight_rows("o", l, c)))
+            O[l, :, :, lo : lo + 2 * HD] = spread(o2.astype(BF16), LR)
+        totals = [scatter_x(nt(some(O, l, h), weight("o", l)), h) for h in range(2)]
         at_b()
-        hidden = X + total() + shift(l, 2)
-        n2, inv2 = norm(hidden)
-        N2[l] = n2
-        I2[l] = inv2
-        HID[...] = hidden
-        Cn[l, t] = (n2 * gain(l, 1) + shift(l, 1)).astype(BF16)
-        wait = gather_x(Cn.at[l])
+        waits = []
+        for h in range(2):
+            rows = halves[h]
+            hidden = HID[rows] + totals[h]() + shift(l, 2)
+            n2, inv2 = norm(hidden)
+            N2[l, rows] = n2
+            I2[l, rows] = inv2
+            HID[rows] = hidden
+            Cn[l, t, rows] = (n2 * gain(l, 1) + shift(l, 1)).astype(BF16)
+            waits.append(gather_x(Cn.at[l], h))
         at_c()
         ready(l, "f")
-        wait()
-        step = F // 2
-        for j in range(2):
-            cols = slice(j * step, (j + 1) * step)
-            u = nn(rows_of(Cn.at[l]), W["f"][l, :, :, :, cols].reshape(D, step)) + pack[l, 6:7, cols]
-            U[l, :, cols] = u
-            Gl[l, :, cols] = gelu(u).astype(BF16)
-        ready(l, "p")
-        total = scatter_x(lambda c: nt(Gl[l], weight_rows("p", l, c)))
+        totals = []
+        for h in range(2):
+            waits[h]()
+            step = F // 2
+            for j in range(2):
+                cols = slice(j * step, (j + 1) * step)
+                u = nn(some(Cn, l, h), W["f"][l, :, :, :, cols].reshape(D, step)) + pack[l, 6:7, cols]
+                U[l, :, halves[h], cols] = spread(u, HR)
+                Gl[l, :, halves[h], cols] = spread(gelu(u).astype(BF16), HR)
+            if h == 0:
+                ready(l, "p")
+            totals.append(scatter_x(nt(some(Gl, l, h), weight("p", l)), h))
         at_d()
-        return (HID[...] + total() + shift(l, 3)) * valid
+        return [
+            lambda h=h: (HID[halves[h]] + totals[h]() + shift(l, 3)) * valid[h] for h in range(2)
+        ]
 
     def grad_matrix(m, l, left, right):
         span = D // Z
@@ -559,41 +572,55 @@
     def column_sum(v):
         return jnp.sum(v, axis=0, keepdims=True)
 
-    def layer_backward(l, dY, at_m, at_c, at_h, at_a):
-        DM[l, t] = dY.astype(BF16)
-        small[l, 5:6, :] = column_sum(dY)
-        wait = gather_x(DM.at[l])
+    def add_small(l, i, h, v):
+        v = column_sum(v)
+        small[l, i : i + 1, :] = v if h == 0 else small[l, i : i + 1, :] + v
+
+    def layer_backward(l, grads_of, at_m, at_c, at_h, at_a):
+        waits = []
+        for h in range(2):
+            dY = grads_of[h]()
+            DYS[halves[h]] = dY
+            DM[l, t, halves[h]] = dY.astype(BF16)
+            waits.append(gather_x(DM.at[l], h))
+            add_small(l, 5, h, dY)
         at_m()
-        wait()
+        totals = []
         step = F // 2
-        for j in range(2):
-            cols = slice(j * step, (j + 1) * step)
-            dg = nn(rows_of(DM.at[l]), W["p"][l, :, :, :, cols].reshape(D, step))
-            DU[:, cols] = (dg * gelu_slope(U[l, :, cols])).astype(BF16)
-        total = scatter_x(lambda c: nt(DU[...], weight_rows("f", l, c)))
-        grad_matrix("p", l, DM.at[l], lambda: Gl[l])
+        for h in range(2):
+            waits[h]()
+            for j in range(2):
+                cols = slice(j * step, (j + 1) * step)
+                dg = nn(some(DM, l, h), W["p"][l, :, :, :, cols].reshape(D, step))
+                du = dg * gelu_slope(some(U, l, h, j * step, (j + 1) * step))
+                DU[:, halves[h], cols] = spread(du.astype(BF16), HR)
+            du = DU[:, halves[h], :].reshape(T * HR, F)
+            totals.append(scatter_x(nt(du, weight("f", l)), h))
+        grad_matrix("p", l, DM.at[l], lambda: every(Gl, l))
         hand_over(l, "p")
-        grad_matrix("f", l, Cn.at[l], lambda: DU[...])
+        grad_matrix("f", l, Cn.at[l], lambda: DU[...].reshape(R, F))
         hand_over(l, "f")
-        small[l, 6:7, :] = column_sum(DU[...].astype(F32))
         at_c()
-        dc = total()
-        dh = dY + norm_back(dc, N2[l], I2[l], gain(l, 1))
-        DH[l, t] = dh.astype(BF16)
-        wait = gather_x(DH.at[l])
-        small[l, 1:2, :] = column_sum(dc * N2[l])
-        small[l, 3:4, :] = column_sum(dc)
-        small[l, 4:5, :] = column_sum(dh)
-        HID[...] = dh
+        waits = []
+        for h in range(2):
+            rows = halves[h]
+            dc = totals[h]()
+            dh = DYS[rows] + norm_back(dc, N2[l, rows], I2[l, rows], gain(l, 1))
+            DH[l, t, rows] = dh.astype(BF16)
+            waits.append(gather_x(DH.at[l], h))
+            HID[rows] = dh
+            add_small(l, 1, h, dc * N2[l, rows])
+            add_small(l, 3, h, dc)
+            add_small(l, 4, h, dh)
+        small[l, 6:7, :F] = column_sum(DU[...].reshape(R, F).astype(F32))
         at_h()
-        wait()
-        DO[...] = nn(rows_of(DH.at[l]), weight("o", l)).astype(BF16)
+        for h in range(2):
+            waits[h]()
+            DO[:, halves[h], :] = spread(nn(some(DH, l, h), weight("o", l)).astype(BF16), HR)
         for pair in range(E // (2 * HD)):
             lo = pair * 2 * HD
-            q2 = QKV[l, :, lo : lo + 2 * HD]
-            k2 = QKV[l, :, E + lo : E + lo + 2 * HD]
-            v2 = QKV[l, :, 2 * E + lo : 2 * E + lo + 2 * HD]
-            do2 = DO[:, lo : lo + 2 * HD]
+            q2, k2, v2 = (every(QKV, l, i * E + lo, i * E + lo + 2 * HD) for i in range(3))
+            do2 = DO[:, :, lo : lo + 2 * HD].reshape(R, 2 * HD)
             dq = dk = dv = None
             for h in range(2):
                 pr = PR[l, pair * 2 + h]
@@ -605,20 +632,27 @@
                     dq, dk, dv = parts
                 else:
                     dq, dk, dv = dq + parts[0], dk + parts[1], dv + parts[2]
-            DQKV[:, lo : lo + 2 * HD] = (dq * factor).astype(BF16)
-            DQKV[:, E + lo : E + lo + 2 * HD] = (dk * factor).astype(BF16)
-            DQKV[:, 2 * E + lo : 2 * E + lo + 2 * HD] = dv.astype(BF16)
-        total = scatter_x(lambda c: nt(DQKV[...], weight_rows("q", l, c)))
-        grad_matrix("q", l, A.at[l], lambda: DQKV[...])
-        grad_matrix("o", l, DH.at[l], lambda: O[l])
+            for i, v in enumerate((dq * factor, dk * factor, dv)):
+                DQKV[:, :, i * E + lo : i * E + lo + 2 * HD] = spread(v.astype(BF16), LR)
+        totals = []
+        for h in range(2):
+            dqkv = DQKV[:, halves[h], :].reshape(T * HR, 3 * E)
+            totals.append(scatter_x(nt(dqkv, weight("q", l)), h))
+        grad_matrix("q", l, A.at[l], lambda: DQKV[...].reshape(R, 3 * E))
+        grad_matrix("o", l, DH.at[l], lambda: every(O, l))
         hand_over(l, "a")
         small[l, 7:8, :] = jnp.zeros((1, D), F32)
-        small[l, 7:8, : 3 * E] = column_sum(DQKV[...].astype(F32))
+        small[l, 7:8, : 3 * E] = column_sum(DQKV[...].reshape(R, 3 * E).astype(F32))
         at_a()
-        da = total()
-        small[l, 0:1, :] = column_sum(da * N1[l])
-        small[l, 2:3, :] = column_sum(da)
-        return HID[...] + norm_back(da, N1[l], I1[l], gain(l, 0))
+
+        def result(h):
+            rows = halves[h]
+            da = totals[h]()
+            add_small(l, 0, h, da * N1[l, rows])
+            add_small(l, 2, h, da)
+            return HID[rows] + norm_back(da, N1[l, rows], I1[l, rows], gain(l, 0))
+
+        return [lambda h=h: result(h) for h in range(2)]
 
     class Small:
         def __init__(self, l):
@@ -705,29 +739,33 @@
     def nothing():
         pass
 
-    y0 = layer_forward(0, x_in[s].astype(F32), f0_a, f0_q, f0_b, f0_c, f0_d)
-    act0 = y0.astype(BF16)
-
-    @pl.when(s == 0)
-    def _():
-        act_out[0] = act0
-
-    @pl.when(s == 1)
-    def _():
-        act_send[...] = act0
-        act_copy.start()
-
-    y1 = layer_forward(1, act0.astype(F32), f1_a, nothing, f1_b, nothing, nothing)
-    act1 = y1.astype(BF16)
-
-    @pl.when(s == 1)
-    def _():
-        act_out[1] = act1
-
-    @pl.when(s == 0)
-    def _():
-        act_send[...] = act1
-        act_copy.start()
+    def keep(core, out, send, h, v):
+        @pl.when(s == core)
+        def _():
+            out[core, halves[h]] = v
+
+        @pl.when(s == 1 - core)
+        def _():
+            send[halves[h]] = v
+
+    def sent(core, move):
+        on(1 - core, move.start)
+
+    x_of = [lambda h=h: x_in[s, halves[h]].astype(F32) for h in range(2)]
+    y0 = layer_forward(0, x_of, f0_a, f0_q, f0_b, f0_c, f0_d)
+
+    def first_output(h):
+        v = y0[h]().astype(BF16)
+        keep(0, act_out, act_send, h, v)
+        return v.astype(F32)
+
+    y0_of = [lambda h=h: first_output(h) for h in range(2)]
+
+    def f1_start():
+        sent(0, act_copy)
+        f1_a()
+
+    y1 = layer_forward(1, y0_of, f1_start, nothing, f1_b, nothing, nothing)
 
     def b1_h():
         task(1, "pr1")
@@ -735,19 +773,24 @@
     def b1_a():
         task(1, "fr1", "pr2")
 
-    ig1 = layer_backward(1, cot_in[s].astype(F32) * valid, nothing, nothing, b1_h, b1_a).astype(BF16)
-    smalls[1].begin()
-
-    @pl.when(s == 1)
-    def _():
-        grad_out[1] = ig1
-
-    @pl.when(s == 0)
-    def _():
-        ig_send[...] = ig1
-        ig_copy.start()
+    def cot_of(h):
+        return cot_in[s, halves[h]].astype(F32) * valid[h]
+
+    def b1_m():
+        for h in range(2):
+            keep(1, act_out, act_send, h, y1[h]().astype(BF16))
+        sent(1, act_copy)
+
+    ig1 = layer_backward(1, [lambda h=h: cot_of(h) for h in range(2)], b1_m, nothing, b1_h, b1_a)
+
+    def ig1_of(h):
+        v = ig1[h]().astype(BF16)
+        keep(1, grad_out, ig_send, h, v)
+        return v.astype(F32) * valid[h]
 
     def b0_m():
+        sent(1, ig_copy)
+        smalls[1].begin()
         task(1, "ar1", "fr2")
         small_task(1, "add")
 
@@ -765,19 +808,13 @@
         task(1, "ar3")
         small_task(1, "over_z")
 
-    ig0 = layer_backward(0, ig1.astype(F32) * valid, b0_m, b0_c, b0_h, b0_a).astype(BF16)
+    ig0 = layer_backward(0, [lambda h=h: ig1_of(h) for h in range(2)], b0_m, b0_c, b0_h, b0_a)
+    task(0, "ar1", "fr2")
+    for h in range(2):
+        keep(0, grad_out, ig_send, h, ig0[h]().astype(BF16))
+    sent(0, ig_copy)
     smalls[0].begin()
 
-    @pl.when(s == 0)
-    def _():
-        grad_out[0] = ig0
-
-    @pl.when(s == 1)
-    def _():
-        ig_send[...] = ig0
-        ig_copy.start()
-
-    task(0, "ar1", "fr2")
     small_task(0, "add")
     small_task(0, "over_x")
     task(0, "pr3", "ar2")
@@ -817,7 +854,7 @@
     names = sz.names
     Z, Y, T, LR, D, E, F, R = sz.Z, sz.Y, sz.T, sz.LR, sz.D, sz.E, sz.F, sz.R
     wd = sz.width
-    n_sems = 168
+    n_sems = 169
     vm = pltpu.VMEM
     scratch = (
         [vm((2, Z, Y, sz.B, wd[m]), BF16) for m in names]
@@ -829,16 +866,16 @@
         + [vm((2, 8, D), F32)]
         + [vm((2, T, LR, D), BF16)] * 4
         + [
-            vm((2, R, 3 * E), BF16),
-            vm((2, R, E), BF16),
+            vm((2, T, LR, 3 * E), BF16),
+            vm((2, T, LR, E), BF16),
             vm((2, E // HD, R, R), BF16),
-            vm((2, R, F), F32),
-            vm((2, R, F), BF16),
+            vm((2, T, LR, F), F32),
+            vm((2, T, LR, F), BF16),
         ]
-        + [vm((R, F), BF16), vm((R, E), BF16), vm((R, 3 * E), BF16)]
+        + [vm((T, LR, F), BF16), vm((T, LR, E), BF16), vm((T, LR, 3 * E), BF16)]
         + [vm((2, LR, D), F32), vm((2, LR, 1), F32), vm((2, LR, D), F32), vm((2, LR, 1), F32)]
-        + [vm((LR, D), F32), vm((R, R), F32)]
-        + [vm((2, sz.C, T, LR, sz.DC), BF16), vm((8, sz.C, T - 1, LR, sz.DC), BF16)]
+        + [vm((LR, D), F32), vm((LR, D), F32), vm((R, R), F32)]
+        + [vm((2, 2, T, sz.HR, D), BF16), vm((8, 2, T - 1, sz.HR, D), BF16)]
         + [
             vm((2, 8, D), F32),
             vm((8, D), F32),

time: 182 us -> 158 us (0.87)
  Pallas kernels: 181 us -> 157 us
    pallas_call x1, Pallas kernels: 178 us -> 154 us  [fused(): pl.pallas_call(body, out_shape=out_shape, in_specs=[spec] * len(arrays),...]
where the time goes in v3:
time: 158 us
  Pallas kernels  157 us (99%)
    pallas_call x1, Pallas kernels, fused(): pl.pallas_call(body, out_shape=out_shape, in_specs=[spec] * len(arrays),...  154 us

profile of v3, /device:TPU:0, one launch (start us, length us, event | category | flops | bytes accessed | tf_op | source)
XLA Modules:
  0.0 157.7 jit_solution(9507280841658182378)
XLA Ops:
  0.6 154.5 %layers.1 = (bf16[2,64,1024]{2,1,0:T(8,128)(2,1)}, bf16[2,64,1024]{2,1,0:T(8,128)(2,1)}, f32[3,64,256]{2,1,0:T(8,128)}, f32[1,768]{1,0:T(1,128)}, f32[64,256]{1,...) custom-call(bf16[2,64,1024]{2,1,0:T(8,128)(2,1)} %refs_0_.1, ...), custom_call_target="tpu_custom_call" | custom-call | tf_op jit(solution)/shard_map/layers/pallas_call | solution.py:894
  155.1 2.4 %hand_out.1 = (bf16[2,64,1024]{2,1,0:T(8,128)(2,1)}, bf16[2,64,1024]{2,1,0:T(8,128)(2,1)}, f32[3,64,256]{2,1,0:T(8,128)}, f32[1,768]{1,0:T(1,128)}, f32[64,256]{...) custom-call(bf16[2,64,1024]{2,1,0:T(8,128)(2,1)} %get-tuple-element., ...), custom_call_target="tpu_custom_call" | custom-call | tf_op jit(solution)/shard_map/hand_out/pallas_call | solution.py:918

commit v4 on v3

--- a/solution.py
+++ b/solution.py
@@ -162,7 +162,7 @@
         [at_x(k) for k in range(1, T)]
         + [at_y(k) for k in range(1, Y)]
         + [at_z(k) for k in range(1, Z)]
-        + [sibling]
+        + [(1 - s, d, (t + k) % T) for k in range(T)]
     )
     for p in peers:
         pl.semaphore_signal(barrier, inc=1, device_id=p, device_id_type=MESH)
@@ -617,6 +617,8 @@
         for h in range(2):
             waits[h]()
             DO[:, halves[h], :] = spread(nn(some(DH, l, h), weight("o", l)).astype(BF16), HR)
+        if l == 0:
+            grad_matrix("o", l, DH.at[l], lambda: every(O, l))
         for pair in range(E // (2 * HD)):
             lo = pair * 2 * HD
             q2, k2, v2 = (every(QKV, l, i * E + lo, i * E + lo + 2 * HD) for i in range(3))
@@ -639,7 +641,8 @@
             dqkv = DQKV[:, halves[h], :].reshape(T * HR, 3 * E)
             totals.append(scatter_x(nt(dqkv, weight("q", l)), h))
         grad_matrix("q", l, A.at[l], lambda: DQKV[...].reshape(R, 3 * E))
-        grad_matrix("o", l, DH.at[l], lambda: every(O, l))
+        if l == 1:
+            grad_matrix("o", l, DH.at[l], lambda: every(O, l))
         hand_over(l, "a")
         small[l, 7:8, :] = jnp.zeros((1, D), F32)
         small[l, 7:8, : 3 * E] = column_sum(DQKV[...].reshape(R, 3 * E).astype(F32))
@@ -658,29 +661,32 @@
         def __init__(self, l):
             self.l = l
             mine = small.at[l]
-            self.over = copy(mine, small_sib, sibling, 1 - l, "small")
-            self.x = [copy(mine, small_x.at[k - 1], at_x(k), l, ("small", 0, k)) for k in far_first(T)]
+            self.over = [
+                copy(mine, small_sib.at[k], (1 - s, d, (t + k) % T), 1 - l, ("small", 3, k))
+                for k in far_first(T) + [0]
+            ]
+            self.x = [
+                copy(mine, small_x.at[k - 1], at_x(k), l, ("small", 0, k)) for k in far_first(T)
+            ]
             self.y = [copy(small_x.at[T - 1], small_y.at[k - 1], at_y(k), l, ("small", 1, k)) for k in far_first(Y)]
             self.z = [copy(small_y.at[Y - 1], small_z.at[k - 1], at_z(k), l, ("small", 2, k)) for k in far_first(Z)]
 
         def begin(self):
-            on(1 - self.l, self.over.start)
-
-        def add(self):
-            l = self.l
-            self.over.wait_recv()
-            small[l] = small[l] + small_sib[...]
-            for c in self.x:
-                c.start()
+            def go(copies):
+                for c in copies:
+                    c.start()
+
+            on(1 - self.l, lambda: go(self.over))
+            on(self.l, lambda: go(self.x))
 
         def over_x(self):
-            for c in self.x:
+            for c in self.x + self.over:
                 c.wait_recv()
-            v = small_x[0]
+            v = small_x[0] + small_sib[1]
             for k in range(1, T - 1):
-                v = v + small_x[k]
+                v = v + small_x[k] + small_sib[k + 1]
             row = lax.broadcasted_iota(jnp.int32, v.shape, 0)
-            small_x[T - 1] = small[self.l] + jnp.where(row < 6, v, 0.0)
+            small_x[T - 1] = small[self.l] + small_sib[0] + jnp.where(row < 6, v, 0.0)
             for c in self.y:
                 c.start()
 
@@ -768,10 +774,10 @@
     y1 = layer_forward(1, y0_of, f1_start, nothing, f1_b, nothing, nothing)
 
     def b1_h():
-        task(1, "pr1")
+        task(1, "pr1", "fr1")
 
     def b1_a():
-        task(1, "fr1", "pr2")
+        task(1, "pr2")
 
     def cot_of(h):
         return cot_in[s, halves[h]].astype(F32) * valid[h]
@@ -792,37 +798,36 @@
         sent(1, ig_copy)
         smalls[1].begin()
         task(1, "ar1", "fr2")
-        small_task(1, "add")
 
     def b0_c():
         task(1, "ar2", "pr3")
         small_task(1, "over_x")
 
     def b0_h():
+        task(0, "pr1", "fr1")
         task(1, "fr3")
         small_task(1, "over_y")
-        task(0, "pr1")
 
     def b0_a():
-        task(0, "fr1", "pr2")
+        task(0, "ar1", "pr2", "fr2")
         task(1, "ar3")
         small_task(1, "over_z")
 
     ig0 = layer_backward(0, [lambda h=h: ig1_of(h) for h in range(2)], b0_m, b0_c, b0_h, b0_a)
-    task(0, "ar1", "fr2")
     for h in range(2):
         keep(0, grad_out, ig_send, h, ig0[h]().astype(BF16))
     sent(0, ig_copy)
     smalls[0].begin()
 
-    small_task(0, "add")
+    task(0, "pr3", "fr3")
     small_task(0, "over_x")
-    task(0, "pr3", "ar2")
+    task(0, "ar2")
     small_task(0, "over_y")
-    task(0, "fr3", "ar3")
+    for l, m in ((1, "a"), (1, "f"), (1, "p"), (0, "p"), (0, "f")):
+        task(l, m + "r4")
+    task(0, "ar3")
     small_task(0, "over_z")
-    for l in range(2):
-        task(l, *(m + "r4" for m in names))
+    task(0, "ar4")
 
     act_copy.wait_recv()
     act_out[1 - s] = act_recv[...]
@@ -854,7 +859,7 @@
     names = sz.names
     Z, Y, T, LR, D, E, F, R = sz.Z, sz.Y, sz.T, sz.LR, sz.D, sz.E, sz.F, sz.R
     wd = sz.width
-    n_sems = 169
+    n_sems = 172
     vm = pltpu.VMEM
     scratch = (
         [vm((2, Z, Y, sz.B, wd[m]), BF16) for m in names]
@@ -878,7 +883,7 @@
         + [vm((2, 2, T, sz.HR, D), BF16), vm((8, 2, T - 1, sz.HR, D), BF16)]
         + [
             vm((2, 8, D), F32),
-            vm((8, D), F32),
+            vm((T, 8, D), F32),
             vm((T, 8, D), F32),
             vm((Y, 8, D), F32),
             vm((Z, 8, D), F32),

time: 158 us -> 154 us (0.975)
  Pallas kernels: 157 us -> 153 us
    pallas_call x1, Pallas kernels: 154 us -> 151 us  [fused(): pl.pallas_call(body, out_shape=out_shape, in_specs=[spec] * len(arrays),...]
where the time goes in v4:
time: 154 us
  Pallas kernels  153 us (99%)
    pallas_call x1, Pallas kernels, fused(): pl.pallas_call(body, out_shape=out_shape, in_specs=[spec] * len(arrays),...  151 us

profile of v4, /device:TPU:0, one launch (start us, length us, event | category | flops | bytes accessed | tf_op | source)
XLA Modules:
  0.0 153.8 jit_solution(5909314533092037425)
XLA Ops:
  0.6 150.5 %layers.1 = (bf16[2,64,1024]{2,1,0:T(8,128)(2,1)}, bf16[2,64,1024]{2,1,0:T(8,128)(2,1)}, f32[3,64,256]{2,1,0:T(8,128)}, f32[1,768]{1,0:T(1,128)}, f32[64,256]{1,...) custom-call(bf16[2,64,1024]{2,1,0:T(8,128)(2,1)} %refs_0_.1, ...), custom_call_target="tpu_custom_call" | custom-call | tf_op jit(solution)/shard_map/layers/pallas_call | solution.py:899
  151.2 2.4 %hand_out.1 = (bf16[2,64,1024]{2,1,0:T(8,128)(2,1)}, bf16[2,64,1024]{2,1,0:T(8,128)(2,1)}, f32[3,64,256]{2,1,0:T(8,128)}, f32[1,768]{1,0:T(1,128)}, f32[64,256]{...) custom-call(bf16[2,64,1024]{2,1,0:T(8,128)(2,1)} %get-tuple-element., ...), custom_call_target="tpu_custom_call" | custom-call | tf_op jit(solution)/shard_map/hand_out/pallas_call | solution.py:923

commit v5 on v4

--- a/solution.py
+++ b/solution.py
@@ -188,6 +188,7 @@
         def __init__(self, l, m):
             w = W[m]
             self.l = l
+            self.direct = (l, m) == (0, "a")
             half = [pl.ds(0, HB), pl.ds(HB, HB)]
 
             def same(view, device, when, *key):
@@ -213,7 +214,10 @@
                         return w.at[l, pl.ds(lo, size), ring[i], half[h]]
 
                 self.one.append([same(own, at_one(k), h, 1, k) for k in far_first(n)])
-                self.two.append({k: same(strip(0), at_two(k), h, 2, k) for k in (1, m_ - 1)})
+                self.two.append({
+                        k: same(strip(0), at_two(k), h, 2, k)
+                        for k in (far_first(m_) if self.direct else (1, m_ - 1))
+                    })
                 self.far.append(
                     {
                         1: same(strip(m_ - 1, 0, n // 2), at_two(1), h, 3, 1),
@@ -249,12 +253,15 @@
 
         def s3(self, h):
             for k, c in self.two[h].items():
+                if k == 2:
+                    continue
                 c.wait_recv()
-                self.far[h][k].start()
+                if not self.direct:
+                    self.far[h][k].start()
                 self.over[h][1 if k != 1 else len(self.over[h]) - 1][0].start()
 
         def s4(self, h):
-            for c in self.far[h].values():
+            for c in [self.two[h][2]] if self.direct else self.far[h].values():
                 c.wait_recv()
             self.over[h][2][0].start()
 
@@ -427,7 +434,7 @@
                 S = nt(q2, half(k2, h)) * factor
                 S = jnp.where(MASK[...] > 0.5, S, -1e30)
                 e = jnp.exp(S - jnp.max(S, axis=-1, keepdims=True))
-                pr = (e / jnp.sum(e, axis=-1, keepdims=True)).astype(BF16)
+                pr = (e * (1.0 / jnp.sum(e, axis=-1, keepdims=True))).astype(BF16)
                 PR[l, pair * 2 + h] = pr
                 part = nn(pr, half(v2, h))
                 o2 = part if o2 is None else o2 + part
@@ -576,13 +583,16 @@
         v = column_sum(v)
         small[l, i : i + 1, :] = v if h == 0 else small[l, i : i + 1, :] + v
 
-    def layer_backward(l, grads_of, at_m, at_c, at_h, at_a):
+    def layer_backward(l, grads_of, early, at_m, at_c, at_h, at_a):
         waits = []
         for h in range(2):
             dY = grads_of[h]()
             DYS[halves[h]] = dY
-            DM[l, t, halves[h]] = dY.astype(BF16)
-            waits.append(gather_x(DM.at[l], h))
+            if early is None:
+                DM[l, t, halves[h]] = dY.astype(BF16)
+                waits.append(gather_x(DM.at[l], h))
+            else:
+                waits.append(early[h])
             add_small(l, 5, h, dY)
         at_m()
         totals = []
@@ -719,7 +729,27 @@
     act_copy = copy(act_send, act_recv, sibling)
     ig_copy = copy(ig_send, ig_recv, sibling)
 
+    def cot_of(h):
+        return cot_in[s, halves[h]].astype(F32) * valid[h]
+
+    early = []
+
+    def gather_cotangent(h):
+        part = DM.at[1, t, pl.ds(h * HR, HR)]
+        DM[1, t, halves[h]] = cot_of(h).astype(BF16)
+        copies = [copy(part, part, at_x(k), None, ("cotangent", h, k)) for k in far_first(T)]
+        for c in copies:
+            c.start()
+
+        def wait():
+            for c in copies:
+                c.wait_recv()
+
+        early.append(wait)
+
     def f0_a():
+        for h in range(2):
+            gather_cotangent(h)
         phase(0, "as2", "fs2", "as3", "ps2", "as4")
 
     def f0_q():
@@ -779,15 +809,12 @@
     def b1_a():
         task(1, "pr2")
 
-    def cot_of(h):
-        return cot_in[s, halves[h]].astype(F32) * valid[h]
-
-    def b1_m():
+    def b1_c():
         for h in range(2):
             keep(1, act_out, act_send, h, y1[h]().astype(BF16))
         sent(1, act_copy)
 
-    ig1 = layer_backward(1, [lambda h=h: cot_of(h) for h in range(2)], b1_m, nothing, b1_h, b1_a)
+    ig1 = layer_backward(1, [lambda h=h: cot_of(h) for h in range(2)], early, nothing, b1_c, b1_h, b1_a)
 
     def ig1_of(h):
         v = ig1[h]().astype(BF16)
@@ -813,7 +840,7 @@
         task(1, "ar3")
         small_task(1, "over_z")
 
-    ig0 = layer_backward(0, [lambda h=h: ig1_of(h) for h in range(2)], b0_m, b0_c, b0_h, b0_a)
+    ig0 = layer_backward(0, [lambda h=h: ig1_of(h) for h in range(2)], None, b0_m, b0_c, b0_h, b0_a)
     for h in range(2):
         keep(0, grad_out, ig_send, h, ig0[h]().astype(BF16))
     sent(0, ig_copy)
@@ -859,7 +886,7 @@
     names = sz.names
     Z, Y, T, LR, D, E, F, R = sz.Z, sz.Y, sz.T, sz.LR, sz.D, sz.E, sz.F, sz.R
     wd = sz.width
-    n_sems = 172
+    n_sems = 180
     vm = pltpu.VMEM
     scratch = (
         [vm((2, Z, Y, sz.B, wd[m]), BF16) for m in names]

time: 154 us -> 147 us (0.955)
  Pallas kernels: 153 us -> 146 us
    pallas_call x1, Pallas kernels: 151 us -> 144 us  [fused(): pl.pallas_call(body, out_shape=out_shape, in_specs=[spec] * len(arrays),...]
where the time goes in v5:
time: 147 us
  Pallas kernels  146 us (99%)
    pallas_call x1, Pallas kernels, fused(): pl.pallas_call(body, out_shape=out_shape, in_specs=[spec] * len(arrays),...  144 us

profile of v5, /device:TPU:0, one launch (start us, length us, event | category | flops | bytes accessed | tf_op | source)
XLA Modules:
  0.0 147.1 jit_solution(17291874398747474227)
XLA Ops:
  0.6 143.8 %layers.1 = (bf16[2,64,1024]{2,1,0:T(8,128)(2,1)}, bf16[2,64,1024]{2,1,0:T(8,128)(2,1)}, f32[3,64,256]{2,1,0:T(8,128)}, f32[1,768]{1,0:T(1,128)}, f32[64,256]{1,...) custom-call(bf16[2,64,1024]{2,1,0:T(8,128)(2,1)} %refs_0_.1, ...), custom_call_target="tpu_custom_call" | custom-call | tf_op jit(solution)/shard_map/layers/pallas_call | solution.py:926
  144.5 2.4 %hand_out.1 = (bf16[2,64,1024]{2,1,0:T(8,128)(2,1)}, bf16[2,64,1024]{2,1,0:T(8,128)(2,1)}, f32[3,64,256]{2,1,0:T(8,128)}, f32[1,768]{1,0:T(1,128)}, f32[64,256]{...) custom-call(bf16[2,64,1024]{2,1,0:T(8,128)(2,1)} %get-tuple-element., ...), custom_call_target="tpu_custom_call" | custom-call | tf_op jit(solution)/shard_map/hand_out/pallas_call | solution.py:950
